TPU v7x, 32 devices: a whole 2x2x4 slice. The times are simulated.
32 devices in a mesh: groups: 2 (over y), seq: 4 (over z), head: 4 (over x, core).
Axes of the slice: x: 2, y: 2, z: 4, core: 2. Of those that a mesh axis runs over, the one named last changes fastest.
Arguments:
- segment_query: bfloat16 [512, 4096], P(('groups', 'seq'), 'head'), parts along dimension 0, may hold values from -8 to 8
- segment_memory: bfloat16 [512, 2, 1024], P(('groups', 'seq'), None, 'head'), parts along dimension 0, may hold values from -8 to 8
- finished_memory: bfloat16 [2048, 2, 1024], P(('groups', 'seq'), None, 'head'), parts along dimension 0, may hold values from -8 to 8
- cache_memory: bfloat16 [32768, 2, 1024], P(('groups', 'seq'), None, 'head'), parts along dimension 0, may hold values from -8 to 8
- block_mask: int32 [4, 128], P('groups', 'seq'), parts along dimension 0, may hold values 0 or 1
- owner_index: int32 [2], P('groups'), parts along dimension 0, may hold values from 0 to 3
- valid_count: int32 [2], P('groups'), parts along dimension 0, may hold values from 1 to 256
- output_weight: bfloat16 [4096, 4096], P('head', 'seq'), may hold values from -0.09375 to 0.09375
Outputs:
- mixed_output: float32 [512, 4096], P(('groups', 'head'), 'seq'), parts along dimension 0
There are 2 independent parts, one for each index of `groups`. A program takes and returns all parts, laid end to end along the dimension named above; an argument that names none is the same for every part. Nothing has to cross between parts.
All inputs are finite; a program needn't handle non-finite values. No bound on the sum of `block_mask` on one device may be relied on, other than what follows from the above.
Results may differ from a plain program's by a relative error of at most 0.0065.
Values may be sent and summed in bfloat16 or wider, within the bound.
A program may use at most 128 MiB of HBM per device.

v0:
```python
import jax
import jax.numpy as jnp
from jax import lax
from jax.sharding import PartitionSpec as P

HD = 128
BLOCK = 128


floor_value = -1e30


def merged(value, axis, join):
    pieces = jax.tree.map(lambda part: lax.all_gather(part, axis), value)
    head = jax.tree.map(lambda part: part[0], pieces)
    tail = jax.tree.map(lambda part: part[1:], pieces)
    running, _ = lax.scan(lambda running, slab: (join(running, slab), None), head, tail)
    return running


def attend(queries, key_rows, value_rows, valid_mask):
    scores = jnp.einsum(
        "rkgd,tkd->rkgt", queries, key_rows, preferred_element_type=jnp.float32
    ) * queries.shape[-1] ** (-0.5)
    allowed = valid_mask[:, None, None, :]
    scores = jnp.where(allowed, scores, floor_value)
    row_peak = jnp.max(scores, axis=-1)
    weights = jnp.where(allowed, jnp.exp(scores - row_peak[..., None]), 0.0)
    row_total = jnp.sum(weights, axis=-1)
    summed = jnp.einsum(
        "rkgt,tkd->rkgd",
        weights.astype(jnp.bfloat16),
        value_rows,
        preferred_element_type=jnp.float32,
    )
    return (row_peak, row_total, summed)


def join(first_part, second_part):
    row_peak = jnp.maximum(first_part[0], second_part[0])
    first_factor = jnp.exp(first_part[0] - row_peak)
    second_factor = jnp.exp(second_part[0] - row_peak)
    row_total = first_part[1] * first_factor + second_part[1] * second_factor
    summed = first_part[2] * first_factor[..., None] + second_part[2] * second_factor[..., None]
    return (row_peak, row_total, summed)


def per_device(
    segment_query,
    segment_memory,
    finished_memory,
    cache_memory,
    block_mask,
    owner_index,
    valid_count,
    output_weight,
):
    queries_flat, fresh_rows = (
        lax.all_gather(segment_query, "seq", axis=0, tiled=True),
        lax.all_gather(segment_memory, "seq", axis=0, tiled=True),
    )
    segment_len = queries_flat.shape[0]
    kv_local = segment_memory.shape[2] // HD
    group_size = queries_flat.shape[1] // (kv_local * HD)
    queries = queries_flat.reshape(segment_len, kv_local, group_size, HD)
    stat_shape = (segment_len, kv_local, group_size)
    empty_state = (
        jnp.full(stat_shape, floor_value, jnp.float32),
        jnp.zeros(stat_shape, jnp.float32),
        jnp.zeros(stat_shape + (HD,), jnp.float32),
    )

    def recent_part(finished_rows, query_rows):
        pairs = jnp.concatenate([finished_rows, fresh_rows], axis=0)
        key_rows = pairs[:, 0].reshape(-1, kv_local, HD)
        value_rows = pairs[:, 1].reshape(-1, kv_local, HD)
        positions = lax.broadcasted_iota(jnp.int32, (1, 2 * segment_len), 1)
        valid_mask = jnp.broadcast_to(
            positions < segment_len + valid_count[0], (query_rows.shape[0], 2 * segment_len)
        )
        return attend(query_rows, key_rows, value_rows, valid_mask)

    start_state = lax.cond(
        lax.axis_index("seq") == owner_index[0],
        lambda: recent_part(finished_memory, queries),
        lambda: empty_state,
    )
    tile_size = min(512, cache_memory.shape[0])
    tile_count = cache_memory.shape[0] // tile_size
    tile_blocks = tile_size // BLOCK
    query_blocks = segment_len // BLOCK
    cache_tiles = cache_memory.reshape(tile_count, tile_size, 2, kv_local, HD)
    mask_tiles = block_mask.reshape(query_blocks, tile_count, tile_blocks).transpose(1, 0, 2)

    def advance(partial_value, inputs):
        tile_rows, tile_mask = inputs
        expanded = jnp.broadcast_to(
            tile_mask[:, None, :, None] > 0, (query_blocks, BLOCK, tile_blocks, BLOCK)
        ).reshape(segment_len, tile_size)
        return (
            join(partial_value, attend(queries, tile_rows[:, 0], tile_rows[:, 1], expanded)),
            None,
        )

    state, ignored = lax.scan(advance, start_state, (cache_tiles, mask_tiles))
    row_peak, row_total, summed = merged(state, "seq", join)
    attended = (summed / row_total[..., None]).astype(jnp.bfloat16).reshape(segment_len, -1)
    return lax.psum_scatter(
        jnp.dot(attended, output_weight, preferred_element_type=jnp.float32),
        "head",
        scatter_dimension=0,
        tiled=True,
    )


def solution(mesh):
    return jax.shard_map(
        per_device,
        mesh=mesh,
        in_specs=(
            P(("groups", "seq"), "head"),
            P(("groups", "seq"), None, "head"),
            P(("groups", "seq"), None, "head"),
            P(("groups", "seq"), None, "head"),
            P("groups", "seq"),
            P("groups"),
            P("groups"),
            P("head", "seq"),
        ),
        out_specs=P(("groups", "head"), "seq"),
        check_vma=False,
    )
```

profile of v0, /device:TPU:0, one launch (start us, length us, event | category | flops | bytes accessed | tf_op | source)
XLA Modules:
  0.0 266.5 jit_solution(16382702717518910027)
XLA Ops:
  8.1 15.8 %all_gather.24 = bf16[256,2,256]{2,1,0:T(2,128)(2,1)S(1)} all-gather(bf16[64,2,256]{2,1,0:T(2,128)(2,1)} %param.15), channel_id=1, replica_groups=mesh['groups'=2,'seq'=4,'head'=4] {'seq'}, dimensions={0}, use_global_device_ids=true | all-gather | bytes 327680 | tf_op jit(solution)/shard_map/all_gather | solution.py:60
  23.9 16.4 %all_gather.25 = bf16[256,1024]{1,0:T(8,128)(2,1)S(1)} all-gather(bf16[64,1024]{1,0:T(8,128)(2,1)} %param.14), channel_id=1, replica_groups=mesh['groups'=2,'seq'=4,'head'=4] {'seq'}, dimensions={0}, use_global_device_ids=true | all-gather | bytes 655360 | tf_op jit(solution)/shard_map/all_gather | solution.py:59
  40.8 11.7 %reshape.61 = bf16[8,512,2,2,128]{4,3,2,1,0:T(2,128)(2,1)} reshape(bf16[4096,2,256]{2,1,0:T(2,128)(2,1)} %param.17) | data formatting | bytes 8388608 | tf_op jit(solution)/shard_map/reshape | solution.py:92
  52.5 9.9 %conditional.1 = (f32[256,2,4]{0,2,1:T(4,128)}, f32[256,2,4]{0,2,1:T(4,128)S(1)}, f32[256,2,4,128]{0,3,2,1:T(8,128)}) conditional(s32[]{:T(128)} %convert_element_type.12, () %tuple.21, (s32[1]{0:T(128)}, bf16[256,2,256]{2,1,0:T(2,128)(2,1)}, bf16[256,2,256]{2,1,0:T(2,128)(2,1)S(1)}, bf16[256,2,4,128]{0,3,2,1:T(8,128)(2,1)S(1)}) %tuple.83), branch_computations={%region_0.0_spmd, %region_1.4_spmd} | conditional | flops 551547392 | bytes 16812072 | solution.py:83
  53.2 0.9 copy.52
  54.1 1.1 copy.51
  55.2 1.0 pad_maximum_fusion
  56.2 1.4 bitcast_reduce_fusion
  57.6 1.8 fusion.3
  59.5 2.9 %fusion.8 = f32[256,2,4,128]{0,3,2,1:T(8,128)} fusion(bf16[512,2,128,1]{0,2,3,1:T(8,128)(2,1)S(1)} %bitcast.173, f32[2,512,256,4]{2,1,3,0:T(8,128)S(1)} %get-tuple-element.195, f32[256,2,4]{0,2,1:T(4,128)} %get-tuple-element.321, pred[512]{0:T(512)(128)(4,1)S(1)} %iota_compare_fusion), kind=kOutput, calls=%fused_computation.10 | convolution fusion | flops 273678336 | bytes 5513728 | tf_op jit(solution)/shard_map/cond/branch_1_fun/rkgt,tkd->rkgd/dot_general | solution.py:30
  62.4 68.8 %while.28 = (s32[]{:T(128)}, f32[256,2,4]{0,2,1:T(4,128)}, f32[256,2,4]{0,2,1:T(4,128)S(1)}, f32[256,2,4,128]{0,3,2,1:T(8,128)}, s32[8,2,4]{2,0,1:T(8,128)S(1)},...) while((s32[]{:T(128)}, f32[256,2,4]{0,2,1:T(4,128)}, ...), condition=%wide.region_7.8_spmd, body=%wide.region_4.7_spmd.sunk | while | flops 551297024 | bytes 18989268 | solution.py:105
  62.9 1.4 constant_dynamic-slice_fusion.8
  65.2 1.0 fusion.56
  66.2 1.3 multiply_add_fusion.2
  67.5 3.5 %fusion.57 = f32[256,2,4,128]{0,3,2,1:T(8,128)} fusion(f32[2,512,256,4]{2,1,3,0:T(8,128)S(1)} %get-tuple-element.299, f32[256,2,4]{0,2,1:T(4,128)S(1)} %get-tuple-element.300, pred[256,512]{0,1:T(8,128)(4,1)S(1)} %copy.103, f32[256,2,4,128]{0,3,2,1:T(8,128)} %get-tuple-element.335, f32[256,2,4]{0,2,1:T(4,128)S(1)} %bitcast.175, ...), kind=kOutput, calls=%fused_computation.28.clone.1 | convolution fusion | flops 274464768 | bytes 6709248 | tf_op jit(solution)/shard_map/while/body/eval_jaxpr/rkgt,tkd->rkgd/dot_general | solution.py:30
  71.5 1.4 constant_dynamic-slice_fusion.8
  73.8 1.0 fusion.56
  74.8 1.3 multiply_add_fusion.2
  76.1 3.5 %fusion.57 = f32[256,2,4,128]{0,3,2,1:T(8,128)} fusion(f32[2,512,256,4]{2,1,3,0:T(8,128)S(1)} %get-tuple-element.299, f32[256,2,4]{0,2,1:T(4,128)S(1)} %get-tuple-element.300, pred[256,512]{0,1:T(8,128)(4,1)S(1)} %copy.103, f32[256,2,4,128]{0,3,2,1:T(8,128)} %get-tuple-element.335, f32[256,2,4]{0,2,1:T(4,128)S(1)} %bitcast.175, ...), kind=kOutput, calls=%fused_computation.28.clone.1 | convolution fusion | flops 274464768 | bytes 6709248 | tf_op jit(solution)/shard_map/while/body/eval_jaxpr/rkgt,tkd->rkgd/dot_general | solution.py:30
  80.1 1.4 constant_dynamic-slice_fusion.8
  81.6 0.8 fusion.55
  82.4 1.0 fusion.56
  83.4 1.3 multiply_add_fusion.2
  84.7 3.5 %fusion.57 = f32[256,2,4,128]{0,3,2,1:T(8,128)} fusion(f32[2,512,256,4]{2,1,3,0:T(8,128)S(1)} %get-tuple-element.299, f32[256,2,4]{0,2,1:T(4,128)S(1)} %get-tuple-element.300, pred[256,512]{0,1:T(8,128)(4,1)S(1)} %copy.103, f32[256,2,4,128]{0,3,2,1:T(8,128)} %get-tuple-element.335, f32[256,2,4]{0,2,1:T(4,128)S(1)} %bitcast.175, ...), kind=kOutput, calls=%fused_computation.28.clone.1 | convolution fusion | flops 274464768 | bytes 6709248 | tf_op jit(solution)/shard_map/while/body/eval_jaxpr/rkgt,tkd->rkgd/dot_general | solution.py:30
  88.7 1.4 constant_dynamic-slice_fusion.8
  90.2 0.8 fusion.55
  91.0 1.0 fusion.56
  92.0 1.3 multiply_add_fusion.2
  93.3 3.5 %fusion.57 = f32[256,2,4,128]{0,3,2,1:T(8,128)} fusion(f32[2,512,256,4]{2,1,3,0:T(8,128)S(1)} %get-tuple-element.299, f32[256,2,4]{0,2,1:T(4,128)S(1)} %get-tuple-element.300, pred[256,512]{0,1:T(8,128)(4,1)S(1)} %copy.103, f32[256,2,4,128]{0,3,2,1:T(8,128)} %get-tuple-element.335, f32[256,2,4]{0,2,1:T(4,128)S(1)} %bitcast.175, ...), kind=kOutput, calls=%fused_computation.28.clone.1 | convolution fusion | flops 274464768 | bytes 6709248 | tf_op jit(solution)/shard_map/while/body/eval_jaxpr/rkgt,tkd->rkgd/dot_general | solution.py:30
  97.3 1.4 constant_dynamic-slice_fusion.8
  98.8 0.8 fusion.55
  99.6 1.0 fusion.56
  100.6 1.3 multiply_add_fusion.2
  101.9 3.5 %fusion.57 = f32[256,2,4,128]{0,3,2,1:T(8,128)} fusion(f32[2,512,256,4]{2,1,3,0:T(8,128)S(1)} %get-tuple-element.299, f32[256,2,4]{0,2,1:T(4,128)S(1)} %get-tuple-element.300, pred[256,512]{0,1:T(8,128)(4,1)S(1)} %copy.103, f32[256,2,4,128]{0,3,2,1:T(8,128)} %get-tuple-element.335, f32[256,2,4]{0,2,1:T(4,128)S(1)} %bitcast.175, ...), kind=kOutput, calls=%fused_computation.28.clone.1 | convolution fusion | flops 274464768 | bytes 6709248 | tf_op jit(solution)/shard_map/while/body/eval_jaxpr/rkgt,tkd->rkgd/dot_general | solution.py:30
  105.9 1.4 constant_dynamic-slice_fusion.8
  107.4 0.8 fusion.55
  108.2 1.0 fusion.56
  109.3 1.3 multiply_add_fusion.2
  110.6 3.5 %fusion.57 = f32[256,2,4,128]{0,3,2,1:T(8,128)} fusion(f32[2,512,256,4]{2,1,3,0:T(8,128)S(1)} %get-tuple-element.299, f32[256,2,4]{0,2,1:T(4,128)S(1)} %get-tuple-element.300, pred[256,512]{0,1:T(8,128)(4,1)S(1)} %copy.103, f32[256,2,4,128]{0,3,2,1:T(8,128)} %get-tuple-element.335, f32[256,2,4]{0,2,1:T(4,128)S(1)} %bitcast.175, ...), kind=kOutput, calls=%fused_computation.28.clone.1 | convolution fusion | flops 274464768 | bytes 6709248 | tf_op jit(solution)/shard_map/while/body/eval_jaxpr/rkgt,tkd->rkgd/dot_general | solution.py:30
  114.6 1.4 constant_dynamic-slice_fusion.8
  116.8 1.0 fusion.56
  117.9 1.3 multiply_add_fusion.2
  119.2 3.5 %fusion.57 = f32[256,2,4,128]{0,3,2,1:T(8,128)} fusion(f32[2,512,256,4]{2,1,3,0:T(8,128)S(1)} %get-tuple-element.299, f32[256,2,4]{0,2,1:T(4,128)S(1)} %get-tuple-element.300, pred[256,512]{0,1:T(8,128)(4,1)S(1)} %copy.103, f32[256,2,4,128]{0,3,2,1:T(8,128)} %get-tuple-element.335, f32[256,2,4]{0,2,1:T(4,128)S(1)} %bitcast.175, ...), kind=kOutput, calls=%fused_computation.28.clone.1 | convolution fusion | flops 274464768 | bytes 6709248 | tf_op jit(solution)/shard_map/while/body/eval_jaxpr/rkgt,tkd->rkgd/dot_general | solution.py:30
  123.2 1.4 constant_dynamic-slice_fusion.8
  124.6 0.8 fusion.55
  125.4 1.0 fusion.56
  126.5 1.3 multiply_add_fusion.2
  127.8 3.5 %fusion.57 = f32[256,2,4,128]{0,3,2,1:T(8,128)} fusion(f32[2,512,256,4]{2,1,3,0:T(8,128)S(1)} %get-tuple-element.299, f32[256,2,4]{0,2,1:T(4,128)S(1)} %get-tuple-element.300, pred[256,512]{0,1:T(8,128)(4,1)S(1)} %copy.103, f32[256,2,4,128]{0,3,2,1:T(8,128)} %get-tuple-element.335, f32[256,2,4]{0,2,1:T(4,128)S(1)} %bitcast.175, ...), kind=kOutput, calls=%fused_computation.28.clone.1 | convolution fusion | flops 274464768 | bytes 6709248 | tf_op jit(solution)/shard_map/while/body/eval_jaxpr/rkgt,tkd->rkgd/dot_general | solution.py:30
  131.3 2.5 copy.58
  133.9 13.4 %all-gather = f32[1024,2,4]{0,2,1:T(4,128)S(1)} all-gather(f32[256,2,4]{0,2,1:T(4,128)} %get-tuple-element.100), channel_id=2, replica_groups=mesh['groups'=2,'seq'=4,'head'=4] {'seq'}, dimensions={0}, use_global_device_ids=true | all-gather | bytes 40960 | tf_op jit(solution)/shard_map/all_gather | solution.py:14
  147.3 13.6 %all-gather.1 = f32[1024,2,4]{0,2,1:T(4,128)S(1)} all-gather(f32[256,2,4]{0,2,1:T(4,128)S(1)} %get-tuple-element.101), channel_id=3, replica_groups=mesh['groups'=2,'seq'=4,'head'=4] {'seq'}, dimensions={0}, use_global_device_ids=true | all-gather | bytes 40960 | tf_op jit(solution)/shard_map/all_gather | solution.py:14
  160.9 52.6 %all-gather.5.cloned.1.call-done = f32[1024,2,4,128]{3,2,1,0:T(4,128)} async-done(((f32[256,2,4,128]{3,2,1,0:T(4,128)}), f32[1024,2,4,128]{3,2,1,0:T(4,128)}) %all-gather.5.cloned.1.call-update) | async-done | bytes 4194320 | tf_op jit(solution)/shard_map/all_gather | solution.py:14
  213.5 4.2 %slice.51 = f32[768,2,4,128]{3,2,1,0:T(4,128)} slice(f32[1024,2,4,128]{3,2,1,0:T(4,128)} %all-gather.5.cloned.1.call-done), slice={[256:1024], [0:2], [0:4], [0:128]} | slice | bytes 6291456 | tf_op jit(solution)/shard_map/slice | solution.py:16
  217.7 13.7 %while.29 = (s32[]{:T(128)}, f32[256,2,4]{0,2,1:T(4,128)S(1)}, f32[256,2,4]{0,2,1:T(4,128)S(1)}, f32[256,2,4,128]{3,2,1,0:T(4,128)S(1)}, f32[3,256,2,4]{1,0,3,2:...) while((s32[]{:T(128)}, f32[256,2,4]{0,2,1:T(4,128)S(1)}, ...), condition=%wide.region_9.10_spmd, body=%wide.region_8.9_spmd.sunk | while | flops 798722 | bytes 3293285 | solution.py:17
  217.9 0.9 copy.107
  218.8 3.5 %fusion.59 = f32[256,2,4,128]{3,2,1,0:T(4,128)S(1)} fusion(f32[3,256,2,4,128]{4,3,2,1,0:T(4,128)} %get-tuple-element.370, s32[]{:T(128)S(6)} %copy.130, f32[256,2,4,128]{3,2,1,0:T(4,128)S(1)} %get-tuple-element.359, f32[256,2,4]{2,1,0:T(2,128)S(1)} %copy.106, f32[256,2,4]{2,1,0:T(2,128)} %copy.107), kind=kLoop, calls=%fused_computation.44.clone.1 | loop fusion | flops 786432 | bytes 3162116 | tf_op jit(solution)/shard_map/while/body/eval_jaxpr/add | solution.py:44
  222.5 0.9 copy.107
  223.4 3.5 %fusion.59 = f32[256,2,4,128]{3,2,1,0:T(4,128)S(1)} fusion(f32[3,256,2,4,128]{4,3,2,1,0:T(4,128)} %get-tuple-element.370, s32[]{:T(128)S(6)} %copy.130, f32[256,2,4,128]{3,2,1,0:T(4,128)S(1)} %get-tuple-element.359, f32[256,2,4]{2,1,0:T(2,128)S(1)} %copy.106, f32[256,2,4]{2,1,0:T(2,128)} %copy.107), kind=kLoop, calls=%fused_computation.44.clone.1 | loop fusion | flops 786432 | bytes 3162116 | tf_op jit(solution)/shard_map/while/body/eval_jaxpr/add | solution.py:44
  227.1 0.9 copy.107
  228.0 3.5 %fusion.59 = f32[256,2,4,128]{3,2,1,0:T(4,128)S(1)} fusion(f32[3,256,2,4,128]{4,3,2,1,0:T(4,128)} %get-tuple-element.370, s32[]{:T(128)S(6)} %copy.130, f32[256,2,4,128]{3,2,1,0:T(4,128)S(1)} %get-tuple-element.359, f32[256,2,4]{2,1,0:T(2,128)S(1)} %copy.106, f32[256,2,4]{2,1,0:T(2,128)} %copy.107), kind=kLoop, calls=%fused_computation.44.clone.1 | loop fusion | flops 786432 | bytes 3162116 | tf_op jit(solution)/shard_map/while/body/eval_jaxpr/add | solution.py:44
  231.6 1.4 divide_convert_fusion
  233.1 1.4 reshape.44
  234.5 1.7 fusion.39
  236.2 23.5 %reduce-scatter.2.cloned.1.call-done = f32[64,1024]{1,0:T(8,128)} async-done(((f32[256,1024]{1,0:T(8,128)}), f32[64,1024]{1,0:T(8,128)}) %reduce-scatter.2.cloned.1.call-update) | async-done | bytes 262160 | tf_op jit(solution)/shard_map/reduce_scatter | solution.py:108
  (79 shorter events, 9.0 us)
Async XLA Ops:
  6.5 227.9 %copy-start = (bf16[1024,1024]{1,0:T(8,128)(2,1)S(1)}, bf16[1024,1024]{1,0:T(8,128)(2,1)}, u32[]{:S(2)}) copy-start(bf16[1024,1024]{1,0:T(8,128)(2,1)} %param.21) | copy-start | bytes 6291460
  6.5 207.0 %all-gather.5.cloned.1.call-start = ((), (), s32[]{:S(2)}) async-start(), calls=%async_computation.2 | async-start | bytes 5242880 | tf_op jit(solution)/shard_map/all_gather | solution.py:14
  133.8 125.9 %reduce-scatter.2.cloned.1.call-start = ((), (), s32[]{:S(2)}) async-start(), calls=%async_computation.1 | async-start | bytes 1310720 | tf_op jit(solution)/shard_map/reduce_scatter | solution.py:108
  213.5 4.2 %slice-start = ((f32[1024,2,4,128]{3,2,1,0:T(4,128)}), f32[256,2,4,128]{3,2,1,0:T(4,128)S(1)}, s32[]{:S(2)}) async-start(f32[1024,2,4,128]{3,2,1,0:T(4,128)} %all-gather.5.cloned.1.call-done), calls=%async_computation.3 | async-start | bytes 2097152 | tf_op jit(solution)/shard_map/slice | solution.py:15
Sparse Core Ops, SparseCore 0:
  134.0 79.5 all-gather.4
  236.3 23.3 reduce-scatter.1
where the time goes:
time: 268 us; the launch traced here: 267 us
  waiting for transfers between devices  76.1 us (28%)
  blocking collectives  59.2 us (22%)
  local copies, waits for them, and re-layouts  42.2 us (16%)
  matrix products  40.4 us (15%)
  other arithmetic  33.4 us (12%)
  between operations  14.3 us (5%)
    all_gather x1, waiting for transfers between devices, merged(): pieces = jax.tree.map(lambda part: lax.all_gather(part, axis), value)  52.6 us
    dot_general x9, matrix products, attend(): jnp.einsum('rkgt,tkd->rkgd', weights.astype(jnp.bfloat16), value_rows, pr...  30.9 us
    all_gather x2, blocking collectives, merged(): pieces = jax.tree.map(lambda part: lax.all_gather(part, axis), value)  27 us
    reduce_scatter x1, waiting for transfers between devices, per_device(): lax.psum_scatter(jnp.dot(attended, output_weight, preferred_element_type=...  23.5 us
    all_gather x1, blocking collectives, per_device(): lax.all_gather(segment_query, 'seq', axis=0, tiled=True)  16.4 us
    all_gather x1, blocking collectives, per_device(): lax.all_gather(segment_memory, 'seq', axis=0, tiled=True)  15.8 us
    dynamic_slice x24, local copies, waits for them, and re-layouts, per_device(): state, ignored = lax.scan(advance, start_state, (cache_tiles, mask_tiles))  11.9 us
    reshape x1, local copies, waits for them, and re-layouts, per_device(): cache_tiles = cache_memory.reshape(tile_count, tile_size, 2, kv_local, HD)  11.7 us
  transfers between devices with their start and end apart: 2, of which 2 were waited for; matrix products, arithmetic and copies ran while one was open for 0% of the time, Pallas kernels for 0%

commit v1 on v0

v1 whole, which is shorter than its diff:
```python
import functools

import jax
import jax.numpy as jnp
from jax import lax
from jax.experimental import pallas as pl
from jax.experimental.pallas import tpu as pltpu
from jax.sharding import PartitionSpec as P

HD = 128
BLOCK = 128
TILE = 8
FLOOR = -1e30
CEIL = -1e29
LOG2E = 1.4426950408889634


def split_matrix(tokens):
    row = lax.broadcasted_iota(jnp.int32, (2 * BLOCK, 2 * tokens), 0)
    col = lax.broadcasted_iota(jnp.int32, (2 * BLOCK, 2 * tokens), 1)
    want = jnp.where(row < BLOCK, 2 * row, 2 * (row - BLOCK) + 1)
    return jnp.where(row % BLOCK < tokens, jnp.where(col == want, 1.0, 0.0), 0.0).astype(jnp.bfloat16)


def stack_rows(pieces, rows):
    if rows % 16 == 0:
        return jnp.concatenate(pieces, axis=0)
    wide = [piece.astype(jnp.float32) for piece in pieces]
    return jnp.concatenate(wide, axis=0).astype(jnp.bfloat16)


def kernel(
    n,
    heads,
    q_ref,
    seg_hbm,
    fin_hbm,
    cache_hbm,
    mask_ref,
    owner_ref,
    valid_ref,
    w_hbm,
    out_ref,
    cache_raw,
    fin_raw,
    seg_raw,
    w_buf,
    k_buf,
    v_buf,
    score_buf,
    q_buf,
    part_send,
    part_recv,
    att_buf,
    proj_send,
    proj_recv,
    local_sem,
    q_send_sem,
    q_recv_sem,
    part_send_sem,
    part_recv_sem,
    att_send_sem,
    att_recv_sem,
    proj_send_sem,
    proj_recv_sem,
):
    me = lax.axis_index("seq")
    my_head = lax.axis_index("head")
    rows, width = q_ref.shape
    kv_heads = k_buf.shape[1] // HD
    group = width // (kv_heads * HD)
    context = cache_raw.shape[0]
    finished = fin_raw.shape[0]
    pieces = 4
    piece = context // pieces

    local = [
        pltpu.make_async_copy(
            cache_hbm.at[pl.ds(i * piece, piece)],
            cache_raw.at[pl.ds(i * piece, piece)],
            local_sem.at[i],
        )
        for i in range(pieces)
    ]
    local.append(pltpu.make_async_copy(fin_hbm, fin_raw, local_sem.at[pieces]))
    local.append(pltpu.make_async_copy(seg_hbm, seg_raw, local_sem.at[pieces + 1]))
    local.append(pltpu.make_async_copy(w_hbm, w_buf, local_sem.at[pieces + 2]))
    for copy in local:
        copy.start()

    barrier = pltpu.get_barrier_semaphore()
    for i in range(1, n):
        pl.semaphore_signal(barrier, inc=1, device_id={"seq": lax.rem(me + i, n)})
    for i in range(1, heads):
        pl.semaphore_signal(barrier, inc=1, device_id={"head": lax.rem(my_head + i, heads)})
    pl.semaphore_wait(barrier, n + heads - 2)

    def q_copy(target, owner):
        return pltpu.make_async_remote_copy(
            src_ref=q_ref,
            dst_ref=q_buf.at[owner],
            send_sem=q_send_sem.at[target],
            recv_sem=q_recv_sem.at[owner],
            device_id={"seq": target},
        )

    def part_copy(target, owner):
        return pltpu.make_async_remote_copy(
            src_ref=part_send.at[target],
            dst_ref=part_recv.at[owner],
            send_sem=part_send_sem.at[target],
            recv_sem=part_recv_sem.at[owner],
            device_id={"seq": target},
        )

    def att_copy(target, owner):
        return pltpu.make_async_remote_copy(
            src_ref=att_buf.at[owner],
            dst_ref=att_buf.at[owner],
            send_sem=att_send_sem.at[target],
            recv_sem=att_recv_sem.at[owner],
            device_id={"seq": target},
        )

    def proj_copy(target, owner):
        return pltpu.make_async_remote_copy(
            src_ref=proj_send.at[target],
            dst_ref=proj_recv.at[owner],
            send_sem=proj_send_sem.at[target],
            recv_sem=proj_recv_sem.at[owner],
            device_id={"head": target},
        )

    for i in range(1, n):
        q_copy(lax.rem(me - i + n, n), me).start()
    q_buf[me] = q_ref[...]

    def part_block(matrix, raw, start):
        pair = raw.reshape(2 * raw.shape[0], raw.shape[2])
        split = jnp.dot(matrix, pair, preferred_element_type=jnp.float32).astype(jnp.bfloat16)
        k_buf[pl.ds(start, BLOCK), :] = split[:BLOCK]
        ones = jnp.ones((BLOCK, HD), jnp.bfloat16)
        for kv in range(kv_heads):
            v_buf[kv, pl.ds(start, BLOCK), pl.ds(0, HD)] = split[BLOCK:, kv * HD : (kv + 1) * HD]
            v_buf[kv, pl.ds(start, BLOCK), pl.ds(HD, HD)] = ones

    full = split_matrix(BLOCK)
    for i in range(pieces):
        local[i].wait()

        def part_cache(step, carry, i=i):
            start = pl.multiple_of(i * piece + step * BLOCK, BLOCK)
            part_block(full, cache_raw[pl.ds(start, BLOCK)], start)
            return carry

        lax.fori_loop(0, piece // BLOCK, part_cache, 0, unroll=4)
    local[pieces].wait()
    for i in range(finished // BLOCK):
        part_block(full, fin_raw[pl.ds(i * BLOCK, BLOCK)], context + i * BLOCK)
    local[pieces + 1].wait()
    part_block(split_matrix(rows), seg_raw[...], context + finished)

    lane = lax.broadcasted_iota(jnp.int32, (1, HD), 1)
    finished_bias = jnp.where(owner_ref[0] == me, 0.0, FLOOR)
    fresh_bias = jnp.where(lane < jnp.minimum(valid_ref[0] - me * rows, rows), 0.0, FLOOR)
    cache_blocks = context // BLOCK
    blocks = cache_blocks + finished // BLOCK + 1
    tiles = [range(i, min(i + TILE, blocks)) for i in range(0, blocks, TILE)]
    scale = LOG2E * HD**-0.5
    lanes = lax.broadcasted_iota(jnp.int32, (rows, HD), 1)

    def attend(step, carry):
        chunk = lax.rem(me + step, n)

        @pl.when(step > 0)
        def _():
            q_copy(chunk, chunk).wait_recv()

        query_block = (chunk * rows) // BLOCK
        biases = [jnp.where(mask_ref[query_block, j] > 0, 0.0, FLOOR) for j in range(cache_blocks)]
        biases += [finished_bias] * (finished // BLOCK) + [fresh_bias]
        queries = [
            stack_rows(
                [q_buf[chunk, :, pl.ds((kv * group + g) * HD, HD)] for g in range(group)], rows
            )
            for kv in range(kv_heads)
        ]
        peaks = [None] * kv_heads
        sums = [None] * kv_heads

        def score_tile(kv, tile):
            start, size = tile[0] * BLOCK, len(tile) * BLOCK
            scores = lax.dot_general(
                queries[kv],
                k_buf[pl.ds(start, size), pl.ds(kv * HD, HD)],
                (((1,), (1,)), ((), ())),
                preferred_element_type=jnp.float32,
            )
            for offset, j in enumerate(tile):
                biased = scores[:, offset * BLOCK : (offset + 1) * BLOCK] * scale + biases[j]
                score_buf[kv, :, pl.ds(j * BLOCK, BLOCK)] = biased
                peaks[kv] = biased if peaks[kv] is None else jnp.maximum(peaks[kv], biased)

        def value_tile(kv, peak, tile):
            start, size = tile[0] * BLOCK, len(tile) * BLOCK
            weights = [
                jnp.exp2(score_buf[kv, :, pl.ds(j * BLOCK, BLOCK)] - peak).astype(jnp.bfloat16)
                for j in tile
            ]
            term = jnp.dot(
                jnp.concatenate(weights, axis=1),
                v_buf[kv, pl.ds(start, size), :],
                preferred_element_type=jnp.float32,
            )
            sums[kv] = term if sums[kv] is None else sums[kv] + term

        logs = jnp.zeros((rows, HD), jnp.float32)
        for tile in tiles:
            score_tile(0, tile)
        for kv in range(kv_heads):
            peak = jnp.maximum(jnp.max(peaks[kv], axis=1, keepdims=True), CEIL)
            for tile in tiles:
                value_tile(kv, peak, tile)
                if kv + 1 < kv_heads:
                    score_tile(kv + 1, tile)
            total = sums[kv][:, HD:]
            some = total > 0.0
            safe = jnp.where(some, total, 1.0)
            log_total = jnp.where(some, peak + jnp.log2(safe), FLOOR)
            mean = (sums[kv][:, :HD] / safe).astype(jnp.bfloat16)
            for g in range(group):
                number = kv * group + g
                part_send[chunk, :, pl.ds(number * HD, HD)] = mean[g * rows : (g + 1) * rows]
                logs = jnp.where(lanes % 32 == number, log_total[g * rows : (g + 1) * rows], logs)
        high = logs.astype(jnp.bfloat16).astype(jnp.float32)
        middle = (logs - high).astype(jnp.bfloat16).astype(jnp.float32)
        low = logs - high - middle
        packed = jnp.where(lanes < 32, high, jnp.where(lanes < 64, middle, low))
        part_send[chunk, :, pl.ds(width, HD)] = packed.astype(jnp.bfloat16)

        @pl.when(step > 0)
        def _():
            part_copy(chunk, me).start()

        return carry

    lax.fori_loop(0, n, attend, 0)

    def unpack(ref):
        packed = ref[:, pl.ds(width, HD)].astype(jnp.float32)
        return packed[:, :32] + packed[:, 32:64] + packed[:, 64:96]

    sources = [part_send.at[me]]
    for i in range(1, n):
        peer = lax.rem(me + n - i, n)
        part_copy(peer, peer).wait_recv()
        sources.append(part_recv.at[peer])
    logs = [unpack(source) for source in sources]
    top = functools.reduce(jnp.maximum, logs)
    factors = [jnp.exp2(value - top) for value in logs]
    inverse = 1.0 / functools.reduce(jnp.add, factors)
    factors = [factor * inverse for factor in factors]
    for number in range(width // HD):
        columns = pl.ds(number * HD, HD)
        terms = [
            source[:, columns].astype(jnp.float32) * factor[:, number : number + 1]
            for source, factor in zip(sources, factors)
        ]
        att_buf[me, :, columns] = functools.reduce(jnp.add, terms).astype(jnp.bfloat16)

    for i in range(1, n):
        att_copy(lax.rem(me - i + n, n), me).start()
    local[pieces + 2].wait()

    share = n // heads
    for i in range(heads):
        target = lax.rem(me // share + i, heads)
        for j in range(share):
            peer = target * share + j

            @pl.when(peer != me)
            def _():
                att_copy(peer, peer).wait_recv()

        attended = stack_rows([att_buf[target * share + j] for j in range(share)], rows)
        product = jnp.dot(attended, w_buf[...], preferred_element_type=jnp.float32)

        @pl.when(target == my_head)
        def _():
            out_ref[...] = product

        @pl.when(target != my_head)
        def _():
            proj_send[target] = product.astype(jnp.bfloat16)
            proj_copy(target, my_head).start()

    for i in range(1, heads):
        peer = lax.rem(my_head + i, heads)
        proj_copy(peer, peer).wait_recv()
        out_ref[...] += proj_recv[peer].astype(jnp.float32)

    for i in range(1, n):
        peer = lax.rem(me + i, n)
        q_copy(peer, me).wait_send()
        part_copy(peer, me).wait_send()
        att_copy(peer, me).wait_send()
    for i in range(1, heads):
        proj_copy(lax.rem(my_head + i, heads), my_head).wait_send()


def per_device(n, heads, *args):
    query, segment, finished, cache, mask, owner, valid, weight = args
    rows, width = query.shape
    kv_width = segment.shape[2]
    kv_heads = kv_width // HD
    total = cache.shape[0] + finished.shape[0] + BLOCK
    out_rows = rows * n // heads
    bf16, f32 = jnp.bfloat16, jnp.float32
    hbm = pl.BlockSpec(memory_space=pl.ANY)
    vmem = pl.BlockSpec(memory_space=pltpu.VMEM)
    smem = pl.BlockSpec(memory_space=pltpu.SMEM)
    dma = pltpu.SemaphoreType.DMA
    return pl.pallas_call(
        functools.partial(kernel, n, heads),
        out_shape=jax.ShapeDtypeStruct((out_rows, weight.shape[1]), f32),
        in_specs=[vmem, hbm, hbm, hbm, smem, smem, smem, hbm],
        out_specs=vmem,
        scratch_shapes=[
            pltpu.VMEM(cache.shape, bf16),
            pltpu.VMEM(finished.shape, bf16),
            pltpu.VMEM(segment.shape, bf16),
            pltpu.VMEM(weight.shape, bf16),
            pltpu.VMEM((total, kv_width), bf16),
            pltpu.VMEM((kv_heads, total, 2 * HD), bf16),
            pltpu.VMEM((kv_heads, rows * width // kv_width, total), f32),
            pltpu.VMEM((n, rows, width), bf16),
            pltpu.VMEM((n, rows, width + HD), bf16),
            pltpu.VMEM((n, rows, width + HD), bf16),
            pltpu.VMEM((n, rows, width), bf16),
            pltpu.VMEM((heads, out_rows, weight.shape[1]), bf16),
            pltpu.VMEM((heads, out_rows, weight.shape[1]), bf16),
            dma((7,)),
            dma((n,)),
            dma((n,)),
            dma((n,)),
            dma((n,)),
            dma((n,)),
            dma((n,)),
            dma((heads,)),
            dma((heads,)),
        ],
        compiler_params=pltpu.CompilerParams(
            collective_id=0, has_side_effects=True, vmem_limit_bytes=56 << 20
        ),
    )(query, segment, finished, cache, mask, owner, valid, weight)


def solution(mesh):
    return jax.shard_map(
        functools.partial(per_device, mesh.shape["seq"], mesh.shape["head"]),
        mesh=mesh,
        in_specs=(
            P(("groups", "seq"), "head"),
            P(("groups", "seq"), None, "head"),
            P(("groups", "seq"), None, "head"),
            P(("groups", "seq"), None, "head"),
            P("groups", "seq"),
            P("groups"),
            P("groups"),
            P("head", "seq"),
        ),
        out_specs=P(("groups", "head"), "seq"),
        check_vma=False,
    )
```

time: 268 us -> 53.8 us (0.20)
  waiting for transfers between devices: 76.1 us -> 0 us
  blocking collectives: 59.2 us -> 0 us
  Pallas kernels: 0 us -> 50.7 us
  local copies, waits for them, and re-layouts: 42.2 us -> 1.67 us
  matrix products: 40.4 us -> 0 us
  other arithmetic: 33.4 us -> 0 us
  between operations: 14.3 us -> 1.3 us
    all_gather x4 -> x0, blocking collectives: 59.2 us -> none  [the longest x2 27 us: merged(): pieces = jax.tree.map(lambda part: lax.all_gather(part, axis), value)]
    all_gather x1 -> x0, waiting for transfers between devices: 52.6 us -> none  [merged(): pieces = jax.tree.map(lambda part: lax.all_gather(part, axis), value)]
    pallas_call x0 -> x1, Pallas kernels: none -> 50.7 us  [per_device(): pl.pallas_call(functools.partial(kernel, n, heads), out_shape=jax.ShapeDt...]
    dot_general x19 -> x0, matrix products: 40.4 us -> none  [the longest x9 30.9 us: attend(): jnp.einsum('rkgt,tkd->rkgd', weights.astype(jnp.bfloat16), value_rows, pr...]
    reduce_scatter x1 -> x0, waiting for transfers between devices: 23.5 us -> none  [per_device(): lax.psum_scatter(jnp.dot(attended, output_weight, preferred_element_type=...]
    add x14 -> x0, other arithmetic: 20.9 us -> none  [the longest x11 10.5 us: join(): row_total = first_part[1] * first_factor + second_part[1] * second_factor]
    reshape x3 -> x0, local copies, waits for them, and re-layouts: 13.9 us -> none  [the longest x1 11.7 us: per_device(): cache_tiles = cache_memory.reshape(tile_count, tile_size, 2, kv_local, HD)]
    dynamic_slice x27 -> x0, local copies, waits for them, and re-layouts: 11.9 us -> none  [the longest x24 11.9 us: per_device(): state, ignored = lax.scan(advance, start_state, (cache_tiles, mask_tiles))]
  transfers between devices with their start and end apart: 2 -> 0, of which waited for: 2 -> 0; matrix products, arithmetic and copies ran while one was open for 0% -> 0% of each run, Pallas kernels for 0% -> 0%
where the time goes in v1:
time: 53.8 us; the launch traced here: 53.6 us
  Pallas kernels  50.7 us (94%)
  local copies, waits for them, and re-layouts  1.67 us (3%)
  between operations  1.3 us (2%)
    pallas_call x1, Pallas kernels, per_device(): pl.pallas_call(functools.partial(kernel, n, heads), out_shape=jax.ShapeDt...  50.7 us
    unnamed x1, local copies, waits for them, and re-layouts  1.67 us

profile of v1, /device:TPU:0, one launch (start us, length us, event | category | flops | bytes accessed | tf_op | source)
XLA Modules:
  0.0 53.6 jit_solution(11948333732594407082)
XLA Ops:
  1.3 50.7 %shard_map.82 = f32[64,1024]{1,0:T(8,128)} custom-call(bf16[64,1024]{1,0:T(8,128)(2,1)} %q_ref.1, bf16[64,2,256]{2,1,0:T(2,128)(2,1)} %seg_hbm.1, bf16[256,2,256]{2,1,0:T(2,128)(2,1)} %fin_hbm.1, bf16[4096,2,256]{2,1,0:T(2,128)(2,1)} %cache_hbm.1, s32[2,32]{1,0:T(2,128)} %mask_ref.1, s32[1]{0:T(128)S(6)} %copy.10.owner_ref, s32[1]{0:T(128)S(6)} %copy.11.valid_ref, ...), custom_call_target="tpu_custom_call" | custom-call | tf_op jit(solution)/shard_map/pallas_call | solution.py:323
  52.0 1.7 %copy.12 = f32[64,1024]{1,0:T(8,128)} copy(f32[64,1024]{1,0:T(8,128)} %shard_map.82) | data formatting | bytes 524288

commit v2 on v1

--- a/solution.py
+++ b/solution.py
@@ -71,6 +71,7 @@
     group = width // (kv_heads * HD)
     context = cache_raw.shape[0]
     finished = fin_raw.shape[0]
+    order = [0, *range(n // 2, n), *range(n // 2 - 1, 0, -1)]
     pieces = 4
     piece = context // pieces
 
@@ -117,7 +118,7 @@
         return pltpu.make_async_remote_copy(
             src_ref=att_buf.at[owner],
             dst_ref=att_buf.at[owner],
-            send_sem=att_send_sem.at[target],
+            send_sem=att_send_sem.at[target ^ owner],
             recv_sem=att_recv_sem.at[owner],
             device_id={"seq": target},
         )
@@ -131,8 +132,8 @@
             device_id={"head": target},
         )
 
-    for i in range(1, n):
-        q_copy(lax.rem(me - i + n, n), me).start()
+    for i in order[1:]:
+        q_copy(me ^ i, me).start()
     q_buf[me] = q_ref[...]
 
     def part_block(matrix, raw, start):
@@ -170,7 +171,8 @@
     lanes = lax.broadcasted_iota(jnp.int32, (rows, HD), 1)
 
     def attend(step, carry):
-        chunk = lax.rem(me + step, n)
+        distance = jnp.where(step < n // 2 + 1, step + n // 2 - 1, n - step)
+        chunk = me ^ jnp.where(step == 0, 0, distance)
 
         @pl.when(step > 0)
         def _():
@@ -251,8 +253,8 @@
         return packed[:, :32] + packed[:, 32:64] + packed[:, 64:96]
 
     sources = [part_send.at[me]]
-    for i in range(1, n):
-        peer = lax.rem(me + n - i, n)
+    for i in order[1:]:
+        peer = me ^ i
         part_copy(peer, peer).wait_recv()
         sources.append(part_recv.at[peer])
     logs = [unpack(source) for source in sources]
@@ -268,19 +270,26 @@
         ]
         att_buf[me, :, columns] = functools.reduce(jnp.add, terms).astype(jnp.bfloat16)
 
-    for i in range(1, n):
-        att_copy(lax.rem(me - i + n, n), me).start()
+    def spread(distance):
+        step = (distance & -distance if distance else n) // 2
+        while step:
+            att_copy(me ^ step, me ^ distance).start()
+            step //= 2
+
+    spread(0)
     local[pieces + 2].wait()
 
     share = n // heads
-    for i in range(heads):
-        target = lax.rem(me // share + i, heads)
-        for j in range(share):
-            peer = target * share + j
-
-            @pl.when(peer != me)
-            def _():
-                att_copy(peer, peer).wait_recv()
+    routes = sorted(range(1, n), key=lambda d: (d.bit_count(), -d))
+    if share > 1:
+        for distance in routes:
+            att_copy(me ^ distance, me ^ distance).wait_recv()
+            spread(distance)
+    for i in [0] + sorted(range(1, heads), key=lambda d: (d.bit_count(), -d)):
+        target = (me // share) ^ i
+        if share == 1 and i > 0:
+            att_copy(me ^ i, me ^ i).wait_recv()
+            spread(i)
 
         attended = stack_rows([att_buf[target * share + j] for j in range(share)], rows)
         product = jnp.dot(attended, w_buf[...], preferred_element_type=jnp.float32)
@@ -303,7 +312,7 @@
         peer = lax.rem(me + i, n)
         q_copy(peer, me).wait_send()
         part_copy(peer, me).wait_send()
-        att_copy(peer, me).wait_send()
+        att_copy(me ^ i, me).wait_send()
     for i in range(1, heads):
         proj_copy(lax.rem(my_head + i, heads), my_head).wait_send()
 

time: 53.8 us -> 49.5 us (0.920)
  Pallas kernels: 50.7 us -> 46.2 us
    pallas_call x1, Pallas kernels: 50.7 us -> 46.2 us  [per_device(): pl.pallas_call(functools.partial(kernel, n, heads), out_shape=jax.ShapeDt...]
where the time goes in v2:
time: 49.5 us; the launch traced here: 49.2 us
  Pallas kernels  46.2 us (93%)
  local copies, waits for them, and re-layouts  1.67 us (3%)
  between operations  1.3 us (3%)
    pallas_call x1, Pallas kernels, per_device(): pl.pallas_call(functools.partial(kernel, n, heads), out_shape=jax.ShapeDt...  46.2 us
    unnamed x1, local copies, waits for them, and re-layouts  1.67 us

profile of v2, /device:TPU:0, one launch (start us, length us, event | category | flops | bytes accessed | tf_op | source)
XLA Modules:
  0.0 49.2 jit_solution(13873662544320347620)
XLA Ops:
  1.3 46.2 %shard_map.82 = f32[64,1024]{1,0:T(8,128)} custom-call(bf16[64,1024]{1,0:T(8,128)(2,1)} %q_ref.1, bf16[64,2,256]{2,1,0:T(2,128)(2,1)} %seg_hbm.1, bf16[256,2,256]{2,1,0:T(2,128)(2,1)} %fin_hbm.1, bf16[4096,2,256]{2,1,0:T(2,128)(2,1)} %cache_hbm.1, s32[2,32]{1,0:T(2,128)} %mask_ref.1, s32[1]{0:T(128)S(6)} %copy.10.owner_ref, s32[1]{0:T(128)S(6)} %copy.11.valid_ref, ...), custom_call_target="tpu_custom_call" | custom-call | tf_op jit(solution)/shard_map/pallas_call | solution.py:332
  47.5 1.7 %copy.12 = f32[64,1024]{1,0:T(8,128)} copy(f32[64,1024]{1,0:T(8,128)} %shard_map.82) | data formatting | bytes 524288

commit v3 on v2

--- a/solution.py
+++ b/solution.py
@@ -9,7 +9,9 @@
 
 HD = 128
 BLOCK = 128
-TILE = 8
+TILE = 4
+DEEP = 8
+PAD = 16
 FLOOR = -1e30
 CEIL = -1e29
 LOG2E = 1.4426950408889634
@@ -140,10 +142,9 @@
         pair = raw.reshape(2 * raw.shape[0], raw.shape[2])
         split = jnp.dot(matrix, pair, preferred_element_type=jnp.float32).astype(jnp.bfloat16)
         k_buf[pl.ds(start, BLOCK), :] = split[:BLOCK]
-        ones = jnp.ones((BLOCK, HD), jnp.bfloat16)
         for kv in range(kv_heads):
-            v_buf[kv, pl.ds(start, BLOCK), pl.ds(0, HD)] = split[BLOCK:, kv * HD : (kv + 1) * HD]
-            v_buf[kv, pl.ds(start, BLOCK), pl.ds(HD, HD)] = ones
+            v_buf[kv, pl.ds(0, HD), pl.ds(start, BLOCK)] = split[BLOCK:, kv * HD : (kv + 1) * HD].T
+            v_buf[kv, pl.ds(HD, PAD), pl.ds(start, BLOCK)] = jnp.ones((PAD, BLOCK), jnp.bfloat16)
 
     full = split_matrix(BLOCK)
     for i in range(pieces):
@@ -161,14 +162,16 @@
     local[pieces + 1].wait()
     part_block(split_matrix(rows), seg_raw[...], context + finished)
 
-    lane = lax.broadcasted_iota(jnp.int32, (1, HD), 1)
+    batch = group * rows
+    token = lax.broadcasted_iota(jnp.int32, (BLOCK, batch), 0)
     finished_bias = jnp.where(owner_ref[0] == me, 0.0, FLOOR)
-    fresh_bias = jnp.where(lane < jnp.minimum(valid_ref[0] - me * rows, rows), 0.0, FLOOR)
+    fresh_bias = jnp.where(token < jnp.minimum(valid_ref[0] - me * rows, rows), 0.0, FLOOR)
     cache_blocks = context // BLOCK
     blocks = cache_blocks + finished // BLOCK + 1
     tiles = [range(i, min(i + TILE, blocks)) for i in range(0, blocks, TILE)]
+    deep_tiles = [range(i, min(i + DEEP, blocks)) for i in range(0, blocks, DEEP)]
     scale = LOG2E * HD**-0.5
-    lanes = lax.broadcasted_iota(jnp.int32, (rows, HD), 1)
+    stat_row = lax.broadcasted_iota(jnp.int32, (PAD, batch), 0)
 
     def attend(step, carry):
         distance = jnp.where(step < n // 2 + 1, step + n // 2 - 1, n - step)
@@ -182,9 +185,13 @@
         biases = [jnp.where(mask_ref[query_block, j] > 0, 0.0, FLOOR) for j in range(cache_blocks)]
         biases += [finished_bias] * (finished // BLOCK) + [fresh_bias]
         queries = [
-            stack_rows(
-                [q_buf[chunk, :, pl.ds((kv * group + g) * HD, HD)] for g in range(group)], rows
-            )
+            jnp.concatenate(
+                [
+                    q_buf[chunk, :, pl.ds((kv * group + g) * HD, HD)].astype(jnp.float32)
+                    for g in range(group)
+                ],
+                axis=0,
+            ).T.astype(jnp.bfloat16)
             for kv in range(kv_heads)
         ]
         peaks = [None] * kv_heads
@@ -192,53 +199,52 @@
 
         def score_tile(kv, tile):
             start, size = tile[0] * BLOCK, len(tile) * BLOCK
-            scores = lax.dot_general(
+            scores = jnp.dot(
+                k_buf[pl.ds(start, size), pl.ds(kv * HD, HD)],
                 queries[kv],
-                k_buf[pl.ds(start, size), pl.ds(kv * HD, HD)],
-                (((1,), (1,)), ((), ())),
                 preferred_element_type=jnp.float32,
             )
             for offset, j in enumerate(tile):
-                biased = scores[:, offset * BLOCK : (offset + 1) * BLOCK] * scale + biases[j]
-                score_buf[kv, :, pl.ds(j * BLOCK, BLOCK)] = biased
-                peaks[kv] = biased if peaks[kv] is None else jnp.maximum(peaks[kv], biased)
+                biased = scores[offset * BLOCK : (offset + 1) * BLOCK] * scale + biases[j]
+                score_buf[kv, pl.ds(j * BLOCK, BLOCK), :] = biased
+                best = jnp.max(biased.reshape(BLOCK // 8, 8, batch), axis=0)
+                peaks[kv] = best if peaks[kv] is None else jnp.maximum(peaks[kv], best)
 
         def value_tile(kv, peak, tile):
             start, size = tile[0] * BLOCK, len(tile) * BLOCK
             weights = [
-                jnp.exp2(score_buf[kv, :, pl.ds(j * BLOCK, BLOCK)] - peak).astype(jnp.bfloat16)
+                jnp.exp2(score_buf[kv, pl.ds(j * BLOCK, BLOCK), :] - peak).astype(jnp.bfloat16)
                 for j in tile
             ]
             term = jnp.dot(
-                jnp.concatenate(weights, axis=1),
-                v_buf[kv, pl.ds(start, size), :],
+                v_buf[kv, :, pl.ds(start, size)],
+                jnp.concatenate(weights, axis=0),
                 preferred_element_type=jnp.float32,
             )
             sums[kv] = term if sums[kv] is None else sums[kv] + term
 
-        logs = jnp.zeros((rows, HD), jnp.float32)
+        stats = jnp.zeros((PAD, batch), jnp.float32)
         for tile in tiles:
             score_tile(0, tile)
         for kv in range(kv_heads):
-            peak = jnp.maximum(jnp.max(peaks[kv], axis=1, keepdims=True), CEIL)
-            for tile in tiles:
+            peak = jnp.maximum(jnp.max(peaks[kv], axis=0, keepdims=True), CEIL)
+            later = list(tiles) if kv + 1 < kv_heads else []
+            for tile in deep_tiles:
                 value_tile(kv, peak, tile)
-                if kv + 1 < kv_heads:
-                    score_tile(kv + 1, tile)
-            total = sums[kv][:, HD:]
+                for ahead in later[: DEEP // TILE]:
+                    score_tile(kv + 1, ahead)
+                later = later[DEEP // TILE :]
+            total = sums[kv][HD : HD + 1]
             some = total > 0.0
             safe = jnp.where(some, total, 1.0)
             log_total = jnp.where(some, peak + jnp.log2(safe), FLOOR)
-            mean = (sums[kv][:, :HD] / safe).astype(jnp.bfloat16)
-            for g in range(group):
-                number = kv * group + g
-                part_send[chunk, :, pl.ds(number * HD, HD)] = mean[g * rows : (g + 1) * rows]
-                logs = jnp.where(lanes % 32 == number, log_total[g * rows : (g + 1) * rows], logs)
-        high = logs.astype(jnp.bfloat16).astype(jnp.float32)
-        middle = (logs - high).astype(jnp.bfloat16).astype(jnp.float32)
-        low = logs - high - middle
-        packed = jnp.where(lanes < 32, high, jnp.where(lanes < 64, middle, low))
-        part_send[chunk, :, pl.ds(width, HD)] = packed.astype(jnp.bfloat16)
+            mean = sums[kv][:HD] * (1.0 / safe)
+            part_send[chunk, pl.ds(kv * HD, HD), :] = mean.astype(jnp.bfloat16)
+            high = log_total.astype(jnp.bfloat16).astype(jnp.float32)
+            middle = (log_total - high).astype(jnp.bfloat16).astype(jnp.float32)
+            for i, value in enumerate((high, middle, log_total - high - middle)):
+                stats = jnp.where(stat_row == 3 * kv + i, value, stats)
+        part_send[chunk, pl.ds(kv_heads * HD, PAD), :] = stats.astype(jnp.bfloat16)
 
         @pl.when(step > 0)
         def _():
@@ -247,28 +253,26 @@
         return carry
 
     lax.fori_loop(0, n, attend, 0)
-
-    def unpack(ref):
-        packed = ref[:, pl.ds(width, HD)].astype(jnp.float32)
-        return packed[:, :32] + packed[:, 32:64] + packed[:, 64:96]
 
     sources = [part_send.at[me]]
     for i in order[1:]:
         peer = me ^ i
         part_copy(peer, peer).wait_recv()
         sources.append(part_recv.at[peer])
-    logs = [unpack(source) for source in sources]
-    top = functools.reduce(jnp.maximum, logs)
-    factors = [jnp.exp2(value - top) for value in logs]
-    inverse = 1.0 / functools.reduce(jnp.add, factors)
-    factors = [factor * inverse for factor in factors]
-    for number in range(width // HD):
-        columns = pl.ds(number * HD, HD)
+    stats = [source[pl.ds(kv_heads * HD, PAD), :].astype(jnp.float32) for source in sources]
+    for kv in range(kv_heads):
+        logs = [jnp.sum(stat[3 * kv : 3 * kv + 3], axis=0, keepdims=True) for stat in stats]
+        top = functools.reduce(jnp.maximum, logs)
+        factors = [jnp.exp2(value - top) for value in logs]
+        inverse = 1.0 / functools.reduce(jnp.add, factors)
         terms = [
-            source[:, columns].astype(jnp.float32) * factor[:, number : number + 1]
+            source[pl.ds(kv * HD, HD), :].astype(jnp.float32) * (factor * inverse)
             for source, factor in zip(sources, factors)
         ]
-        att_buf[me, :, columns] = functools.reduce(jnp.add, terms).astype(jnp.bfloat16)
+        merged = functools.reduce(jnp.add, terms).T
+        for g in range(group):
+            columns = pl.ds((kv * group + g) * HD, HD)
+            att_buf[me, :, columns] = merged[g * rows : (g + 1) * rows].astype(jnp.bfloat16)
 
     def spread(distance):
         step = (distance & -distance if distance else n) // 2
@@ -323,6 +327,7 @@
     kv_width = segment.shape[2]
     kv_heads = kv_width // HD
     total = cache.shape[0] + finished.shape[0] + BLOCK
+    batch = rows * width // kv_width
     out_rows = rows * n // heads
     bf16, f32 = jnp.bfloat16, jnp.float32
     hbm = pl.BlockSpec(memory_space=pl.ANY)
@@ -340,11 +345,11 @@
             pltpu.VMEM(segment.shape, bf16),
             pltpu.VMEM(weight.shape, bf16),
             pltpu.VMEM((total, kv_width), bf16),
-            pltpu.VMEM((kv_heads, total, 2 * HD), bf16),
-            pltpu.VMEM((kv_heads, rows * width // kv_width, total), f32),
+            pltpu.VMEM((kv_heads, HD + PAD, total), bf16),
+            pltpu.VMEM((kv_heads, total, batch), f32),
             pltpu.VMEM((n, rows, width), bf16),
-            pltpu.VMEM((n, rows, width + HD), bf16),
-            pltpu.VMEM((n, rows, width + HD), bf16),
+            pltpu.VMEM((n, kv_width + PAD, batch), bf16),
+            pltpu.VMEM((n, kv_width + PAD, batch), bf16),
             pltpu.VMEM((n, rows, width), bf16),
             pltpu.VMEM((heads, out_rows, weight.shape[1]), bf16),
             pltpu.VMEM((heads, out_rows, weight.shape[1]), bf16),

time: 49.5 us -> 49.5 us (level)
  no operation moved by 1% of the time
where the time goes in v3:
time: 49.5 us; the launch traced here: 49.1 us
  Pallas kernels  46.1 us (93%)
  local copies, waits for them, and re-layouts  1.67 us (3%)
  between operations  1.3 us (3%)
    pallas_call x1, Pallas kernels, per_device(): pl.pallas_call(functools.partial(kernel, n, heads), out_shape=jax.ShapeDt...  46.1 us
    unnamed x1, local copies, waits for them, and re-layouts  1.67 us

profile of v3, /device:TPU:0, one launch (start us, length us, event | category | flops | bytes accessed | tf_op | source)
XLA Modules:
  0.0 49.1 jit_solution(4841706043977385838)
XLA Ops:
  1.3 46.1 %shard_map.82 = f32[64,1024]{1,0:T(8,128)} custom-call(bf16[64,1024]{1,0:T(8,128)(2,1)} %q_ref.1, bf16[64,2,256]{2,1,0:T(2,128)(2,1)} %seg_hbm.1, bf16[256,2,256]{2,1,0:T(2,128)(2,1)} %fin_hbm.1, bf16[4096,2,256]{2,1,0:T(2,128)(2,1)} %cache_hbm.1, s32[2,32]{1,0:T(2,128)} %mask_ref.1, s32[1]{0:T(128)S(6)} %copy.10.owner_ref, s32[1]{0:T(128)S(6)} %copy.11.valid_ref, ...), custom_call_target="tpu_custom_call" | custom-call | tf_op jit(solution)/shard_map/pallas_call | solution.py:337
  47.4 1.7 %copy.12 = f32[64,1024]{1,0:T(8,128)} copy(f32[64,1024]{1,0:T(8,128)} %shard_map.82) | data formatting | bytes 524288

commit v4 on v3

v4 whole, which is shorter than its diff:
```python
import functools

import jax
import jax.numpy as jnp
from jax import lax
from jax.experimental import pallas as pl
from jax.experimental.pallas import tpu as pltpu
from jax.sharding import PartitionSpec as P

HD = 128
BLOCK = 128
TILE = 8
PAD = 16
FLOOR = -1e30
CEIL = -1e29
LOG2E = 1.4426950408889634


def split_matrix(tokens):
    row = lax.broadcasted_iota(jnp.int32, (2 * BLOCK, 2 * tokens), 0)
    col = lax.broadcasted_iota(jnp.int32, (2 * BLOCK, 2 * tokens), 1)
    want = jnp.where(row < BLOCK, 2 * row, 2 * (row - BLOCK) + 1)
    return jnp.where(row % BLOCK < tokens, jnp.where(col == want, 1.0, 0.0), 0.0).astype(jnp.bfloat16)


def stack_rows(pieces, rows):
    if rows % 16 == 0:
        return jnp.concatenate(pieces, axis=0)
    wide = [piece.astype(jnp.float32) for piece in pieces]
    return jnp.concatenate(wide, axis=0).astype(jnp.bfloat16)


def kernel(
    n,
    heads,
    q_ref,
    seg_hbm,
    fin_hbm,
    cache_hbm,
    mask_ref,
    owner_ref,
    valid_ref,
    w_hbm,
    out_ref,
    cache_raw,
    fin_raw,
    seg_raw,
    w_buf,
    k_buf,
    v_buf,
    score_buf,
    q_buf,
    part_send,
    part_recv,
    att_buf,
    prod_buf,
    proj_send,
    proj_recv,
    local_sem,
    q_send_sem,
    q_recv_sem,
    part_send_sem,
    part_recv_sem,
    att_send_sem,
    att_recv_sem,
    proj_send_sem,
    proj_recv_sem,
):
    me = lax.axis_index("seq")
    my_head = lax.axis_index("head")
    rows, width = q_ref.shape
    kv_heads = k_buf.shape[1] // HD
    group = width // (kv_heads * HD)
    context = cache_raw.shape[0]
    finished = fin_raw.shape[0]
    order = [0, *range(n // 2, n), *range(1, n // 2)]
    pieces = 4
    piece = context // pieces

    local = [
        pltpu.make_async_copy(
            cache_hbm.at[pl.ds(i * piece, piece)],
            cache_raw.at[pl.ds(i * piece, piece)],
            local_sem.at[i],
        )
        for i in range(pieces)
    ]
    local.append(pltpu.make_async_copy(fin_hbm, fin_raw, local_sem.at[pieces]))
    local.append(pltpu.make_async_copy(seg_hbm, seg_raw, local_sem.at[pieces + 1]))
    local.append(pltpu.make_async_copy(w_hbm, w_buf, local_sem.at[pieces + 2]))
    for copy in local:
        copy.start()

    chunk_width = width // kv_heads
    for kv in range(kv_heads):
        q_buf[kv, me] = q_ref[:, pl.ds(kv * chunk_width, chunk_width)]

    barrier = pltpu.get_barrier_semaphore()
    for i in range(1, n):
        pl.semaphore_signal(barrier, inc=1, device_id={"seq": lax.rem(me + i, n)})
    for i in range(1, heads):
        pl.semaphore_signal(barrier, inc=1, device_id={"head": lax.rem(my_head + i, heads)})
    pl.semaphore_wait(barrier, n + heads - 2)

    def seq_copy(source, target_buf, sems, kv, mark, target, owner):
        return pltpu.make_async_remote_copy(
            src_ref=source,
            dst_ref=target_buf.at[kv, owner],
            send_sem=sems[0].at[kv, mark],
            recv_sem=sems[1].at[kv, owner],
            device_id={"seq": target},
        )

    def q_copy(kv, target, owner, mark):
        sems = (q_send_sem, q_recv_sem)
        return seq_copy(q_buf.at[kv, owner], q_buf, sems, kv, mark, target, owner)

    def part_copy(kv, target, owner, mark):
        sems = (part_send_sem, part_recv_sem)
        return seq_copy(part_send.at[kv, target], part_recv, sems, kv, mark, target, owner)

    def att_copy(kv, target, owner, mark):
        sems = (att_send_sem, att_recv_sem)
        return seq_copy(att_buf.at[kv, owner], att_buf, sems, kv, mark, target, owner)

    def proj_copy(target, owner):
        return pltpu.make_async_remote_copy(
            src_ref=proj_send.at[target],
            dst_ref=proj_recv.at[owner],
            send_sem=proj_send_sem.at[target],
            recv_sem=proj_recv_sem.at[owner],
            device_id={"head": target},
        )

    bits = [n >> (i + 1) for i in range(n.bit_length() - 1)]
    for kv in range(kv_heads):
        for bit in bits:
            q_copy(kv, me ^ bit, me, bit).start()

    def part_block(matrix, raw, start):
        pair = raw.reshape(2 * raw.shape[0], raw.shape[2])
        split = jnp.dot(matrix, pair, preferred_element_type=jnp.float32).astype(jnp.bfloat16)
        k_buf[pl.ds(start, BLOCK), :] = split[:BLOCK]
        for kv in range(kv_heads):
            v_buf[kv, pl.ds(0, HD), pl.ds(start, BLOCK)] = split[BLOCK:, kv * HD : (kv + 1) * HD].T
            v_buf[kv, pl.ds(HD, PAD), pl.ds(start, BLOCK)] = jnp.ones((PAD, BLOCK), jnp.bfloat16)

    full = split_matrix(BLOCK)
    for i in range(pieces):
        local[i].wait()

        def part_cache(step, carry, i=i):
            start = pl.multiple_of(i * piece + step * BLOCK, BLOCK)
            part_block(full, cache_raw[pl.ds(start, BLOCK)], start)
            return carry

        lax.fori_loop(0, piece // BLOCK, part_cache, 0, unroll=4)
    local[pieces].wait()
    for i in range(finished // BLOCK):
        part_block(full, fin_raw[pl.ds(i * BLOCK, BLOCK)], context + i * BLOCK)
    local[pieces + 1].wait()
    part_block(split_matrix(rows), seg_raw[...], context + finished)

    batch = group * rows
    token = lax.broadcasted_iota(jnp.int32, (BLOCK, batch), 0)
    finished_bias = jnp.where(owner_ref[0] == me, 0.0, FLOOR)
    fresh_bias = jnp.where(token < jnp.minimum(valid_ref[0] - me * rows, rows), 0.0, FLOOR)
    cache_blocks = context // BLOCK
    blocks = cache_blocks + finished // BLOCK + 1
    tiles = [range(i, min(i + TILE, blocks)) for i in range(0, blocks, TILE)]
    scale = LOG2E * HD**-0.5
    stat_row = lax.broadcasted_iota(jnp.int32, (PAD, batch), 0)

    def attend(kv, step, carry):
        distance = jnp.where(step < n // 2 + 1, step + n // 2 - 1, step - n // 2)
        distance = jnp.where(step == 0, 0, distance)
        chunk = me ^ distance

        @pl.when(step > 0)
        def _():
            q_copy(kv, chunk, chunk, distance).wait_recv()

        for bit in bits[1:]:

            @pl.when((step > 0) & (distance % (2 * bit) == 0))
            def _():
                q_copy(kv, me ^ bit, chunk, distance + bit).start()

        query_block = (chunk * rows) // BLOCK
        biases = [jnp.where(mask_ref[query_block, j] > 0, 0.0, FLOOR) for j in range(cache_blocks)]
        biases += [finished_bias] * (finished // BLOCK) + [fresh_bias]
        queries = jnp.concatenate(
            [q_buf[kv, chunk, :, pl.ds(g * HD, HD)].astype(jnp.float32) for g in range(group)],
            axis=0,
        ).T.astype(jnp.bfloat16)

        def score_tile(tile):
            start, size = tile[0] * BLOCK, len(tile) * BLOCK
            scores = jnp.dot(
                k_buf[pl.ds(start, size), pl.ds(kv * HD, HD)],
                queries,
                preferred_element_type=jnp.float32,
            )
            peak = jnp.full((8, batch), CEIL, jnp.float32)
            for offset, j in enumerate(tile):
                biased = scores[offset * BLOCK : (offset + 1) * BLOCK] * scale + biases[j]
                score_buf[pl.ds(j * BLOCK, BLOCK), :] = biased
                peak = jnp.maximum(peak, jnp.max(biased.reshape(BLOCK // 8, 8, batch), axis=0))
            return jnp.max(peak, axis=0, keepdims=True)

        def value_tile(peak, tile):
            start, size = tile[0] * BLOCK, len(tile) * BLOCK
            weights = [
                jnp.exp2(score_buf[pl.ds(j * BLOCK, BLOCK), :] - peak).astype(jnp.bfloat16)
                for j in tile
            ]
            return jnp.dot(
                v_buf[kv, :, pl.ds(start, size)],
                jnp.concatenate(weights, axis=0),
                preferred_element_type=jnp.float32,
            )

        next_peak = score_tile(tiles[0])
        peak, summed = next_peak, None
        for number, tile in enumerate(tiles):
            tile_peak = next_peak
            if number + 1 < len(tiles):
                next_peak = score_tile(tiles[number + 1])
            term = value_tile(tile_peak, tile)
            if summed is None:
                summed = term
            else:
                joined = jnp.maximum(peak, tile_peak)
                summed = summed * jnp.exp2(peak - joined) + term * jnp.exp2(tile_peak - joined)
                peak = joined
        total = summed[HD : HD + 1]
        some = total > 0.0
        safe = jnp.where(some, total, 1.0)
        log_total = jnp.where(some, peak + jnp.log2(safe), FLOOR)
        part_send[kv, chunk, pl.ds(0, HD), :] = (summed[:HD] * (1.0 / safe)).astype(jnp.bfloat16)
        high = log_total.astype(jnp.bfloat16).astype(jnp.float32)
        middle = (log_total - high).astype(jnp.bfloat16).astype(jnp.float32)
        stats = jnp.zeros((PAD, batch), jnp.float32)
        for i, value in enumerate((high, middle, log_total - high - middle)):
            stats = jnp.where(stat_row == i, value, stats)
        part_send[kv, chunk, pl.ds(HD, PAD), :] = stats.astype(jnp.bfloat16)

        @pl.when(step > 0)
        def _():
            part_copy(kv, chunk, me, distance).start()

        if kv > 0:

            @pl.when(step == n // 2)
            def _():
                merge(kv - 1)

        return carry

    def spread(kv, distance):
        step = (distance & -distance if distance else n) // 2
        while step:
            att_copy(kv, me ^ step, me ^ distance, distance + step).start()
            step //= 2

    def merge(kv):
        sources = [part_send.at[kv, me]]
        for i in order[1:]:
            peer = me ^ i
            part_copy(kv, peer, peer, i).wait_recv()
            sources.append(part_recv.at[kv, peer])
        logs = [
            jnp.sum(source[pl.ds(HD, PAD), :].astype(jnp.float32)[:3], axis=0, keepdims=True)
            for source in sources
        ]
        top = functools.reduce(jnp.maximum, logs)
        factors = [jnp.exp2(value - top) for value in logs]
        inverse = 1.0 / functools.reduce(jnp.add, factors)
        terms = [
            source[pl.ds(0, HD), :].astype(jnp.float32) * (factor * inverse)
            for source, factor in zip(sources, factors)
        ]
        merged = functools.reduce(jnp.add, terms).T
        for g in range(group):
            columns = pl.ds(g * HD, HD)
            att_buf[kv, me, :, columns] = merged[g * rows : (g + 1) * rows].astype(jnp.bfloat16)
        spread(kv, 0)

    for kv in range(kv_heads):
        lax.fori_loop(0, n, functools.partial(attend, kv), 0)

    share = n // heads
    last = kv_heads - 1
    arrived = set()

    def collect(kv, distance):
        if distance and (kv, distance) not in arrived:
            arrived.add((kv, distance))
            att_copy(kv, me ^ distance, me ^ distance, distance).wait_recv()
            spread(kv, distance)

    def collect_all(kv):
        for distance in sorted(range(1, n), key=lambda d: (d.bit_count(), -d)):
            collect(kv, distance)

    def project(kv, i):
        target = (me // share) ^ i
        if share == 1:
            collect(kv, i)
        else:
            collect_all(kv)
        attended = stack_rows([att_buf[kv, target * share + j] for j in range(share)], rows)
        product = jnp.dot(
            attended,
            w_buf[pl.ds(kv * chunk_width, chunk_width), :],
            preferred_element_type=jnp.float32,
        )
        if kv > 0:
            product = product + prod_buf[i]
        if kv < last:
            prod_buf[i] = product
            return

        @pl.when(target == my_head)
        def _():
            out_ref[...] = product

        @pl.when(target != my_head)
        def _():
            proj_send[target] = product.astype(jnp.bfloat16)
            proj_copy(target, my_head).start()

    local[pieces + 2].wait()

    head_order = [0] + sorted(range(1, heads), key=lambda d: (d.bit_count(), -d))
    for kv in range(last):
        collect(kv, n // 2)
        project(kv, 0)
    merge(last)
    for kv in range(last):
        for i in head_order[1:]:
            project(kv, i)
    for i in head_order:
        project(last, i)

    for i in range(1, heads):
        peer = lax.rem(my_head + i, heads)
        proj_copy(peer, peer).wait_recv()
        out_ref[...] += proj_recv[peer].astype(jnp.float32)

    for kv in range(kv_heads):
        for i in range(1, n):
            q_copy(kv, me ^ i, me, i).wait_send()
            part_copy(kv, me ^ i, me, i).wait_send()
            att_copy(kv, me ^ i, me, i).wait_send()
    for i in range(1, heads):
        proj_copy(lax.rem(my_head + i, heads), my_head).wait_send()


def per_device(n, heads, *args):
    query, segment, finished, cache, mask, owner, valid, weight = args
    rows, width = query.shape
    kv_width = segment.shape[2]
    kv_heads = kv_width // HD
    total = cache.shape[0] + finished.shape[0] + BLOCK
    batch = rows * width // kv_width
    out_rows = rows * n // heads
    bf16, f32 = jnp.bfloat16, jnp.float32
    hbm = pl.BlockSpec(memory_space=pl.ANY)
    vmem = pl.BlockSpec(memory_space=pltpu.VMEM)
    smem = pl.BlockSpec(memory_space=pltpu.SMEM)
    dma = pltpu.SemaphoreType.DMA
    return pl.pallas_call(
        functools.partial(kernel, n, heads),
        out_shape=jax.ShapeDtypeStruct((out_rows, weight.shape[1]), f32),
        in_specs=[vmem, hbm, hbm, hbm, smem, smem, smem, hbm],
        out_specs=vmem,
        scratch_shapes=[
            pltpu.VMEM(cache.shape, bf16),
            pltpu.VMEM(finished.shape, bf16),
            pltpu.VMEM(segment.shape, bf16),
            pltpu.VMEM(weight.shape, bf16),
            pltpu.VMEM((total, kv_width), bf16),
            pltpu.VMEM((kv_heads, HD + PAD, total), bf16),
            pltpu.VMEM((total, batch), f32),
            pltpu.VMEM((kv_heads, n, rows, width // kv_heads), bf16),
            pltpu.VMEM((kv_heads, n, HD + PAD, batch), bf16),
            pltpu.VMEM((kv_heads, n, HD + PAD, batch), bf16),
            pltpu.VMEM((kv_heads, n, rows, width // kv_heads), bf16),
            pltpu.VMEM((heads, out_rows, weight.shape[1]), f32),
            pltpu.VMEM((heads, out_rows, weight.shape[1]), bf16),
            pltpu.VMEM((heads, out_rows, weight.shape[1]), bf16),
            dma((7,)),
            dma((kv_heads, n)),
            dma((kv_heads, n)),
            dma((kv_heads, n)),
            dma((kv_heads, n)),
            dma((kv_heads, n)),
            dma((kv_heads, n)),
            dma((heads,)),
            dma((heads,)),
        ],
        compiler_params=pltpu.CompilerParams(
            collective_id=0, has_side_effects=True, vmem_limit_bytes=56 << 20
        ),
    )(query, segment, finished, cache, mask, owner, valid, weight)


def solution(mesh):
    return jax.shard_map(
        functools.partial(per_device, mesh.shape["seq"], mesh.shape["head"]),
        mesh=mesh,
        in_specs=(
            P(("groups", "seq"), "head"),
            P(("groups", "seq"), None, "head"),
            P(("groups", "seq"), None, "head"),
            P(("groups", "seq"), None, "head"),
            P("groups", "seq"),
            P("groups"),
            P("groups"),
            P("head", "seq"),
        ),
        out_specs=P(("groups", "head"), "seq"),
        check_vma=False,
    )
```

time: 49.5 us -> 48.1 us (0.972)
  Pallas kernels: 46.1 us -> 45 us
    pallas_call x1, Pallas kernels: 46.1 us -> 45 us  [per_device(): pl.pallas_call(functools.partial(kernel, n, heads), out_shape=jax.ShapeDt...]
where the time goes in v4:
time: 48.1 us; the launch traced here: 48 us
  Pallas kernels  45 us (94%)
  local copies, waits for them, and re-layouts  1.67 us (3%)
  between operations  1.3 us (3%)
    pallas_call x1, Pallas kernels, per_device(): pl.pallas_call(functools.partial(kernel, n, heads), out_shape=jax.ShapeDt...  45 us
    unnamed x1, local copies, waits for them, and re-layouts  1.67 us

profile of v4, /device:TPU:0, one launch (start us, length us, event | category | flops | bytes accessed | tf_op | source)
XLA Modules:
  0.0 48.0 jit_solution(6708055433138621976)
XLA Ops:
  1.3 45.0 %shard_map.82 = f32[64,1024]{1,0:T(8,128)} custom-call(bf16[64,1024]{1,0:T(8,128)(2,1)} %q_ref.1, bf16[64,2,256]{2,1,0:T(2,128)(2,1)} %seg_hbm.1, bf16[256,2,256]{2,1,0:T(2,128)(2,1)} %fin_hbm.1, bf16[4096,2,256]{2,1,0:T(2,128)(2,1)} %cache_hbm.1, s32[2,32]{1,0:T(2,128)} %mask_ref.1, s32[1]{0:T(128)S(6)} %copy.10.owner_ref, s32[1]{0:T(128)S(6)} %copy.11.valid_ref, ...), custom_call_target="tpu_custom_call" | custom-call | tf_op jit(solution)/shard_map/pallas_call | solution.py:373
  46.3 1.7 %copy.12 = f32[64,1024]{1,0:T(8,128)} copy(f32[64,1024]{1,0:T(8,128)} %shard_map.82) | data formatting | bytes 524288

commit v5 on v4

--- a/solution.py
+++ b/solution.py
@@ -10,6 +10,7 @@
 HD = 128
 BLOCK = 128
 TILE = 8
+SUB = 2
 PAD = 16
 FLOOR = -1e30
 CEIL = -1e29
@@ -69,7 +70,8 @@
     me = lax.axis_index("seq")
     my_head = lax.axis_index("head")
     rows, width = q_ref.shape
-    kv_heads = k_buf.shape[1] // HD
+    kv_heads = k_buf.shape[0]
+    query_blocks = mask_ref.shape[0]
     group = width // (kv_heads * HD)
     context = cache_raw.shape[0]
     finished = fin_raw.shape[0]
@@ -137,36 +139,47 @@
         for bit in bits:
             q_copy(kv, me ^ bit, me, bit).start()
 
-    def part_block(matrix, raw, start):
+    def part_block(matrix, raw, start, biases):
         pair = raw.reshape(2 * raw.shape[0], raw.shape[2])
         split = jnp.dot(matrix, pair, preferred_element_type=jnp.float32).astype(jnp.bfloat16)
-        k_buf[pl.ds(start, BLOCK), :] = split[:BLOCK]
+        extra = jnp.zeros((BLOCK, HD), jnp.float32)
+        for number, bias in enumerate(biases):
+            extra = jnp.where(lane == number, bias, extra)
+        extra = extra.astype(jnp.bfloat16)
         for kv in range(kv_heads):
+            k_buf[kv, pl.ds(start, BLOCK), pl.ds(0, HD)] = split[:BLOCK, kv * HD : (kv + 1) * HD]
+            k_buf[kv, pl.ds(start, BLOCK), pl.ds(HD, HD)] = extra
             v_buf[kv, pl.ds(0, HD), pl.ds(start, BLOCK)] = split[BLOCK:, kv * HD : (kv + 1) * HD].T
             v_buf[kv, pl.ds(HD, PAD), pl.ds(start, BLOCK)] = jnp.ones((PAD, BLOCK), jnp.bfloat16)
 
+    lane = lax.broadcasted_iota(jnp.int32, (BLOCK, HD), 1)
+    token = lax.broadcasted_iota(jnp.int32, (BLOCK, HD), 0)
+    finished_bias = jnp.where(owner_ref[0] == me, 0.0, FLOOR)
+    fresh_bias = jnp.where(token < jnp.minimum(valid_ref[0] - me * rows, rows), 0.0, FLOOR)
     full = split_matrix(BLOCK)
     for i in range(pieces):
         local[i].wait()
 
         def part_cache(step, carry, i=i):
             start = pl.multiple_of(i * piece + step * BLOCK, BLOCK)
-            part_block(full, cache_raw[pl.ds(start, BLOCK)], start)
+            number = i * (piece // BLOCK) + step
+            biases = [
+                jnp.where(mask_ref[row, number] > 0, 0.0, FLOOR) for row in range(query_blocks)
+            ]
+            part_block(full, cache_raw[pl.ds(start, BLOCK)], start, biases)
             return carry
 
         lax.fori_loop(0, piece // BLOCK, part_cache, 0, unroll=4)
     local[pieces].wait()
     for i in range(finished // BLOCK):
-        part_block(full, fin_raw[pl.ds(i * BLOCK, BLOCK)], context + i * BLOCK)
+        start = context + i * BLOCK
+        part_block(full, fin_raw[pl.ds(i * BLOCK, BLOCK)], start, [finished_bias] * query_blocks)
     local[pieces + 1].wait()
-    part_block(split_matrix(rows), seg_raw[...], context + finished)
+    start = context + finished
+    part_block(split_matrix(rows), seg_raw[...], start, [fresh_bias] * query_blocks)
 
     batch = group * rows
-    token = lax.broadcasted_iota(jnp.int32, (BLOCK, batch), 0)
-    finished_bias = jnp.where(owner_ref[0] == me, 0.0, FLOOR)
-    fresh_bias = jnp.where(token < jnp.minimum(valid_ref[0] - me * rows, rows), 0.0, FLOOR)
-    cache_blocks = context // BLOCK
-    blocks = cache_blocks + finished // BLOCK + 1
+    blocks = (context + finished) // BLOCK + 1
     tiles = [range(i, min(i + TILE, blocks)) for i in range(0, blocks, TILE)]
     scale = LOG2E * HD**-0.5
     stat_row = lax.broadcasted_iota(jnp.int32, (PAD, batch), 0)
@@ -187,56 +200,61 @@
                 q_copy(kv, me ^ bit, chunk, distance + bit).start()
 
         query_block = (chunk * rows) // BLOCK
-        biases = [jnp.where(mask_ref[query_block, j] > 0, 0.0, FLOOR) for j in range(cache_blocks)]
-        biases += [finished_bias] * (finished // BLOCK) + [fresh_bias]
         queries = jnp.concatenate(
             [q_buf[kv, chunk, :, pl.ds(g * HD, HD)].astype(jnp.float32) for g in range(group)],
             axis=0,
-        ).T.astype(jnp.bfloat16)
-
-        def score_tile(tile):
+        ).T
+        mark = lax.broadcasted_iota(jnp.int32, (HD, batch), 0) == query_block
+        queries = jnp.concatenate([queries, jnp.where(mark, 1.0, 0.0)], axis=0)
+        queries = queries.astype(jnp.bfloat16)
+
+        def score_tile(peak, tile):
             start, size = tile[0] * BLOCK, len(tile) * BLOCK
             scores = jnp.dot(
-                k_buf[pl.ds(start, size), pl.ds(kv * HD, HD)],
-                queries,
+                k_buf[kv, pl.ds(start, size), :], queries, preferred_element_type=jnp.float32
+            )
+            score_buf[pl.ds(start, size), :] = scores
+            return jnp.maximum(peak, jnp.max(scores.reshape(size // 8, 8, batch), axis=0))
+
+        def value_tile(peak, tile):
+            start, size = tile[0] * BLOCK, len(tile) * BLOCK
+            weights = jnp.exp2((score_buf[pl.ds(start, size), :] - peak) * scale)
+            return jnp.dot(
+                v_buf[kv, :, pl.ds(start, size)],
+                weights.astype(jnp.bfloat16),
                 preferred_element_type=jnp.float32,
             )
-            peak = jnp.full((8, batch), CEIL, jnp.float32)
-            for offset, j in enumerate(tile):
-                biased = scores[offset * BLOCK : (offset + 1) * BLOCK] * scale + biases[j]
-                score_buf[pl.ds(j * BLOCK, BLOCK), :] = biased
-                peak = jnp.maximum(peak, jnp.max(biased.reshape(BLOCK // 8, 8, batch), axis=0))
-            return jnp.max(peak, axis=0, keepdims=True)
-
-        def value_tile(peak, tile):
-            start, size = tile[0] * BLOCK, len(tile) * BLOCK
-            weights = [
-                jnp.exp2(score_buf[pl.ds(j * BLOCK, BLOCK), :] - peak).astype(jnp.bfloat16)
-                for j in tile
-            ]
-            return jnp.dot(
-                v_buf[kv, :, pl.ds(start, size)],
-                jnp.concatenate(weights, axis=0),
-                preferred_element_type=jnp.float32,
-            )
-
-        next_peak = score_tile(tiles[0])
-        peak, summed = next_peak, None
+
+        def cut(tile):
+            return [tile[i : i + SUB] for i in range(0, len(tile), SUB)]
+
+        floor = jnp.full((8, batch), CEIL, jnp.float32)
+        ahead = floor
+        for part in cut(tiles[0]):
+            ahead = score_tile(ahead, part)
+        peak, summed = None, None
         for number, tile in enumerate(tiles):
-            tile_peak = next_peak
-            if number + 1 < len(tiles):
-                next_peak = score_tile(tiles[number + 1])
-            term = value_tile(tile_peak, tile)
+            tile_peak = jnp.max(ahead, axis=0, keepdims=True)
+            ahead, later = floor, cut(tiles[number + 1]) if number + 1 < len(tiles) else []
+            term = None
+            for part in cut(tile):
+                if later:
+                    ahead = score_tile(ahead, later.pop(0))
+                piece_term = value_tile(tile_peak, part)
+                term = piece_term if term is None else term + piece_term
+            for part in later:
+                ahead = score_tile(ahead, part)
             if summed is None:
-                summed = term
+                peak, summed = tile_peak, term
             else:
                 joined = jnp.maximum(peak, tile_peak)
-                summed = summed * jnp.exp2(peak - joined) + term * jnp.exp2(tile_peak - joined)
+                old, new = jnp.exp2((peak - joined) * scale), jnp.exp2((tile_peak - joined) * scale)
+                summed = summed * old + term * new
                 peak = joined
         total = summed[HD : HD + 1]
         some = total > 0.0
         safe = jnp.where(some, total, 1.0)
-        log_total = jnp.where(some, peak + jnp.log2(safe), FLOOR)
+        log_total = jnp.where(some, peak * scale + jnp.log2(safe), FLOOR)
         part_send[kv, chunk, pl.ds(0, HD), :] = (summed[:HD] * (1.0 / safe)).astype(jnp.bfloat16)
         high = log_total.astype(jnp.bfloat16).astype(jnp.float32)
         middle = (log_total - high).astype(jnp.bfloat16).astype(jnp.float32)
@@ -380,7 +398,7 @@
             pltpu.VMEM(finished.shape, bf16),
             pltpu.VMEM(segment.shape, bf16),
             pltpu.VMEM(weight.shape, bf16),
-            pltpu.VMEM((total, kv_width), bf16),
+            pltpu.VMEM((kv_heads, total, 2 * HD), bf16),
             pltpu.VMEM((kv_heads, HD + PAD, total), bf16),
             pltpu.VMEM((total, batch), f32),
             pltpu.VMEM((kv_heads, n, rows, width // kv_heads), bf16),

time: 48.1 us -> 48.4 us (level)
  no operation moved by 1% of the time
where the time goes in v5:
time: 48.4 us; the launch traced here: 48.2 us
  Pallas kernels  45.2 us (93%)
  local copies, waits for them, and re-layouts  1.67 us (3%)
  between operations  1.3 us (3%)
    pallas_call x1, Pallas kernels, per_device(): pl.pallas_call(functools.partial(kernel, n, heads), out_shape=jax.ShapeDt...  45.2 us
    unnamed x1, local copies, waits for them, and re-layouts  1.67 us

profile of v5, /device:TPU:0, one launch (start us, length us, event | category | flops | bytes accessed | tf_op | source)
XLA Modules:
  0.0 48.2 jit_solution(7071751479290207702)
XLA Ops:
  1.3 45.2 %shard_map.82 = f32[64,1024]{1,0:T(8,128)} custom-call(bf16[64,1024]{1,0:T(8,128)(2,1)} %q_ref.1, bf16[64,2,256]{2,1,0:T(2,128)(2,1)} %seg_hbm.1, bf16[256,2,256]{2,1,0:T(2,128)(2,1)} %fin_hbm.1, bf16[4096,2,256]{2,1,0:T(2,128)(2,1)} %cache_hbm.1, s32[2,32]{1,0:T(2,128)} %mask_ref.1, s32[1]{0:T(128)S(6)} %copy.10.owner_ref, s32[1]{0:T(128)S(6)} %copy.11.valid_ref, ...), custom_call_target="tpu_custom_call" | custom-call | tf_op jit(solution)/shard_map/pallas_call | solution.py:391
  46.5 1.7 %copy.12 = f32[64,1024]{1,0:T(8,128)} copy(f32[64,1024]{1,0:T(8,128)} %shard_map.82) | data formatting | bytes 524288

commit v6 on v5

--- a/solution.py
+++ b/solution.py
@@ -117,13 +117,40 @@
         sems = (q_send_sem, q_recv_sem)
         return seq_copy(q_buf.at[kv, owner], q_buf, sems, kv, mark, target, owner)
 
-    def part_copy(kv, target, owner, mark):
-        sems = (part_send_sem, part_recv_sem)
-        return seq_copy(part_send.at[kv, target], part_recv, sems, kv, mark, target, owner)
-
-    def att_copy(kv, target, owner, mark):
-        sems = (att_send_sem, att_recv_sem)
-        return seq_copy(att_buf.at[kv, owner], att_buf, sems, kv, mark, target, owner)
+    half = n // 2
+
+    def keeper(chunk):
+        return jnp.where(chunk < half, half - 1, half)
+
+    def part_copy(kv, chunk, source):
+        slot = lax.rem(chunk, half)
+        return pltpu.make_async_remote_copy(
+            src_ref=part_send.at[kv, chunk],
+            dst_ref=part_recv.at[kv, slot, source],
+            send_sem=part_send_sem.at[kv, chunk],
+            recv_sem=part_recv_sem.at[kv, slot, source],
+            device_id={"seq": keeper(chunk)},
+        )
+
+    def att_copy(kv, chunk, side):
+        return pltpu.make_async_remote_copy(
+            src_ref=att_buf.at[kv, chunk],
+            dst_ref=att_buf.at[kv, chunk],
+            send_sem=att_send_sem.at[side, kv, chunk],
+            recv_sem=att_recv_sem.at[kv, chunk],
+            device_id={"seq": lax.rem(me + (n - 1 if side == 0 else 1), n)},
+        )
+
+    def att_sides(chunk):
+        middle = keeper(chunk)
+        return ((me <= middle) & (me > 0), (me >= middle) & (me < n - 1))
+
+    def spread(kv, chunk):
+        for side, goes in enumerate(att_sides(chunk)):
+
+            @pl.when(goes)
+            def _():
+                att_copy(kv, chunk, side).start()
 
     def proj_copy(target, owner):
         return pltpu.make_async_remote_copy(
@@ -263,9 +290,9 @@
             stats = jnp.where(stat_row == i, value, stats)
         part_send[kv, chunk, pl.ds(HD, PAD), :] = stats.astype(jnp.bfloat16)
 
-        @pl.when(step > 0)
-        def _():
-            part_copy(kv, chunk, me, distance).start()
+        @pl.when(keeper(chunk) != me)
+        def _():
+            part_copy(kv, chunk, me).start()
 
         if kv > 0:
 
@@ -275,18 +302,18 @@
 
         return carry
 
-    def spread(kv, distance):
-        step = (distance & -distance if distance else n) // 2
-        while step:
-            att_copy(kv, me ^ step, me ^ distance, distance + step).start()
-            step //= 2
-
     def merge(kv):
-        sources = [part_send.at[kv, me]]
+        @pl.when((me == half - 1) | (me == half))
+        def _():
+            for slot in range(half):
+                merge_slot(kv, me - lax.rem(me, half) + slot, slot)
+
+    def merge_slot(kv, chunk, slot):
+        sources = [part_send.at[kv, chunk]]
         for i in order[1:]:
             peer = me ^ i
-            part_copy(kv, peer, peer, i).wait_recv()
-            sources.append(part_recv.at[kv, peer])
+            part_copy(kv, chunk, peer).wait_recv()
+            sources.append(part_recv.at[kv, slot, peer])
         logs = [
             jnp.sum(source[pl.ds(HD, PAD), :].astype(jnp.float32)[:3], axis=0, keepdims=True)
             for source in sources
@@ -301,8 +328,8 @@
         merged = functools.reduce(jnp.add, terms).T
         for g in range(group):
             columns = pl.ds(g * HD, HD)
-            att_buf[kv, me, :, columns] = merged[g * rows : (g + 1) * rows].astype(jnp.bfloat16)
-        spread(kv, 0)
+            att_buf[kv, chunk, :, columns] = merged[g * rows : (g + 1) * rows].astype(jnp.bfloat16)
+        spread(kv, chunk)
 
     for kv in range(kv_heads):
         lax.fori_loop(0, n, functools.partial(attend, kv), 0)
@@ -312,21 +339,20 @@
     arrived = set()
 
     def collect(kv, distance):
-        if distance and (kv, distance) not in arrived:
-            arrived.add((kv, distance))
-            att_copy(kv, me ^ distance, me ^ distance, distance).wait_recv()
-            spread(kv, distance)
-
-    def collect_all(kv):
-        for distance in sorted(range(1, n), key=lambda d: (d.bit_count(), -d)):
-            collect(kv, distance)
+        if (kv, distance) in arrived:
+            return
+        arrived.add((kv, distance))
+        chunk = me ^ distance
+
+        @pl.when(keeper(chunk) != me)
+        def _():
+            att_copy(kv, chunk, 0).wait_recv()
+            spread(kv, chunk)
 
     def project(kv, i):
         target = (me // share) ^ i
-        if share == 1:
-            collect(kv, i)
-        else:
-            collect_all(kv)
+        for j in range(share):
+            collect(kv, i * share + j)
         attended = stack_rows([att_buf[kv, target * share + j] for j in range(share)], rows)
         product = jnp.dot(
             attended,
@@ -350,16 +376,13 @@
 
     local[pieces + 2].wait()
 
-    head_order = [0] + sorted(range(1, heads), key=lambda d: (d.bit_count(), -d))
     for kv in range(last):
-        collect(kv, n // 2)
-        project(kv, 0)
+        for distance in range(n - 1, -1, -1):
+            collect(kv, distance)
     merge(last)
-    for kv in range(last):
-        for i in head_order[1:]:
+    for kv in range(kv_heads):
+        for i in range(heads):
             project(kv, i)
-    for i in head_order:
-        project(last, i)
 
     for i in range(1, heads):
         peer = lax.rem(my_head + i, heads)
@@ -369,8 +392,18 @@
     for kv in range(kv_heads):
         for i in range(1, n):
             q_copy(kv, me ^ i, me, i).wait_send()
-            part_copy(kv, me ^ i, me, i).wait_send()
-            att_copy(kv, me ^ i, me, i).wait_send()
+        for chunk in range(n):
+
+            @pl.when(keeper(chunk) != me)
+            def _():
+                part_copy(kv, chunk, me).wait_send()
+
+            for side, goes in enumerate(att_sides(chunk)):
+
+                @pl.when(goes)
+                def _():
+                    att_copy(kv, chunk, side).wait_send()
+
     for i in range(1, heads):
         proj_copy(lax.rem(my_head + i, heads), my_head).wait_send()
 
@@ -403,7 +436,7 @@
             pltpu.VMEM((total, batch), f32),
             pltpu.VMEM((kv_heads, n, rows, width // kv_heads), bf16),
             pltpu.VMEM((kv_heads, n, HD + PAD, batch), bf16),
-            pltpu.VMEM((kv_heads, n, HD + PAD, batch), bf16),
+            pltpu.VMEM((kv_heads, n // 2, n, HD + PAD, batch), bf16),
             pltpu.VMEM((kv_heads, n, rows, width // kv_heads), bf16),
             pltpu.VMEM((heads, out_rows, weight.shape[1]), f32),
             pltpu.VMEM((heads, out_rows, weight.shape[1]), bf16),
@@ -412,8 +445,8 @@
             dma((kv_heads, n)),
             dma((kv_heads, n)),
             dma((kv_heads, n)),
-            dma((kv_heads, n)),
-            dma((kv_heads, n)),
+            dma((kv_heads, n // 2, n)),
+            dma((2, kv_heads, n)),
             dma((kv_heads, n)),
             dma((heads,)),
             dma((heads,)),

time: 48.4 us -> 52 us (1.074)
  Pallas kernels: 45.2 us -> 48.9 us
    pallas_call x1, Pallas kernels: 45.2 us -> 48.9 us  [per_device(): pl.pallas_call(functools.partial(kernel, n, heads), out_shape=jax.ShapeDt...]
where the time goes in v6:
time: 52 us; the launch traced here: 51.9 us
  Pallas kernels  48.9 us (94%)
  local copies, waits for them, and re-layouts  1.67 us (3%)
  between operations  1.3 us (2%)
    pallas_call x1, Pallas kernels, per_device(): pl.pallas_call(functools.partial(kernel, n, heads), out_shape=jax.ShapeDt...  48.9 us
    unnamed x1, local copies, waits for them, and re-layouts  1.67 us

profile of v6, /device:TPU:0, one launch (start us, length us, event | category | flops | bytes accessed | tf_op | source)
XLA Modules:
  0.0 51.9 jit_solution(13554080403414098918)
XLA Ops:
  1.3 48.9 %shard_map.82 = f32[64,1024]{1,0:T(8,128)} custom-call(bf16[64,1024]{1,0:T(8,128)(2,1)} %q_ref.1, bf16[64,2,256]{2,1,0:T(2,128)(2,1)} %seg_hbm.1, bf16[256,2,256]{2,1,0:T(2,128)(2,1)} %fin_hbm.1, bf16[4096,2,256]{2,1,0:T(2,128)(2,1)} %cache_hbm.1, s32[2,32]{1,0:T(2,128)} %mask_ref.1, s32[1]{0:T(128)S(6)} %copy.10.owner_ref, s32[1]{0:T(128)S(6)} %copy.11.valid_ref, ...), custom_call_target="tpu_custom_call" | custom-call | tf_op jit(solution)/shard_map/pallas_call | solution.py:424
  50.2 1.7 %copy.12 = f32[64,1024]{1,0:T(8,128)} copy(f32[64,1024]{1,0:T(8,128)} %shard_map.82) | data formatting | bytes 524288

commit v7 on v5

--- a/solution.py
+++ b/solution.py
@@ -321,6 +321,20 @@
         for distance in sorted(range(1, n), key=lambda d: (d.bit_count(), -d)):
             collect(kv, distance)
 
+    def project_early():
+        out_rows = out_ref.shape[0]
+        for kv in range(last):
+            collect_all(kv)
+            flat = stack_rows([att_buf[kv, j] for j in range(n)], rows)
+            product = jnp.dot(
+                flat,
+                w_buf[pl.ds(kv * chunk_width, chunk_width), :],
+                preferred_element_type=jnp.float32,
+            )
+            for i in range(heads):
+                part = product[i * out_rows : (i + 1) * out_rows]
+                prod_buf[i] = part if kv == 0 else prod_buf[i] + part
+
     def project(kv, i):
         target = (me // share) ^ i
         if share == 1:
@@ -333,11 +347,8 @@
             w_buf[pl.ds(kv * chunk_width, chunk_width), :],
             preferred_element_type=jnp.float32,
         )
-        if kv > 0:
-            product = product + prod_buf[i]
-        if kv < last:
-            prod_buf[i] = product
-            return
+        if last > 0:
+            product = product + prod_buf[target]
 
         @pl.when(target == my_head)
         def _():
@@ -353,11 +364,8 @@
     head_order = [0] + sorted(range(1, heads), key=lambda d: (d.bit_count(), -d))
     for kv in range(last):
         collect(kv, n // 2)
-        project(kv, 0)
     merge(last)
-    for kv in range(last):
-        for i in head_order[1:]:
-            project(kv, i)
+    project_early()
     for i in head_order:
         project(last, i)
 

time: 48.4 us -> 48.4 us (level)
  no operation moved by 1% of the time
where the time goes in v7:
time: 48.4 us; the launch traced here: 48.2 us
  Pallas kernels  45.2 us (93%)
  local copies, waits for them, and re-layouts  1.67 us (3%)
  between operations  1.3 us (3%)
    pallas_call x1, Pallas kernels, per_device(): pl.pallas_call(functools.partial(kernel, n, heads), out_shape=jax.ShapeDt...  45.2 us
    unnamed x1, local copies, waits for them, and re-layouts  1.67 us

profile of v7, /device:TPU:0, one launch (start us, length us, event | category | flops | bytes accessed | tf_op | source)
XLA Modules:
  0.0 48.2 jit_solution(13433836453042968156)
XLA Ops:
  1.3 45.2 %shard_map.82 = f32[64,1024]{1,0:T(8,128)} custom-call(bf16[64,1024]{1,0:T(8,128)(2,1)} %q_ref.1, bf16[64,2,256]{2,1,0:T(2,128)(2,1)} %seg_hbm.1, bf16[256,2,256]{2,1,0:T(2,128)(2,1)} %fin_hbm.1, bf16[4096,2,256]{2,1,0:T(2,128)(2,1)} %cache_hbm.1, s32[2,32]{1,0:T(2,128)} %mask_ref.1, s32[1]{0:T(128)S(6)} %copy.10.owner_ref, s32[1]{0:T(128)S(6)} %copy.11.valid_ref, ...), custom_call_target="tpu_custom_call" | custom-call | tf_op jit(solution)/shard_map/pallas_call | solution.py:399
  46.5 1.7 %copy.12 = f32[64,1024]{1,0:T(8,128)} copy(f32[64,1024]{1,0:T(8,128)} %shard_map.82) | data formatting | bytes 524288

commit v8 on v7

--- a/solution.py
+++ b/solution.py
@@ -184,7 +184,8 @@
     scale = LOG2E * HD**-0.5
     stat_row = lax.broadcasted_iota(jnp.int32, (PAD, batch), 0)
 
-    def attend(kv, step, carry):
+    def attend(kv, turn, carry):
+        step = turn if kv == 0 else lax.rem(turn + 1, n)
         distance = jnp.where(step < n // 2 + 1, step + n // 2 - 1, step - n // 2)
         distance = jnp.where(step == 0, 0, distance)
         chunk = me ^ distance
@@ -269,7 +270,7 @@
 
         if kv > 0:
 
-            @pl.when(step == n // 2)
+            @pl.when(turn == n // 2)
             def _():
                 merge(kv - 1)
 

time: 48.4 us -> 48.4 us (level); the launches traced: 48.2 us -> 47.5 us
  Pallas kernels: 45.2 us -> 44.6 us
    pallas_call x1, Pallas kernels: 45.2 us -> 44.6 us  [per_device(): pl.pallas_call(functools.partial(kernel, n, heads), out_shape=jax.ShapeDt...]
where the time goes in v8:
time: 48.4 us; the launch traced here: 47.5 us
  Pallas kernels  44.6 us (92%)
  local copies, waits for them, and re-layouts  1.67 us (3%)
  between operations  1.3 us (3%)
    pallas_call x1, Pallas kernels, per_device(): pl.pallas_call(functools.partial(kernel, n, heads), out_shape=jax.ShapeDt...  44.6 us
    unnamed x1, local copies, waits for them, and re-layouts  1.67 us

profile of v8, /device:TPU:0, one launch (start us, length us, event | category | flops | bytes accessed | tf_op | source)
XLA Modules:
  0.0 47.5 jit_solution(1969556674763542791)
XLA Ops:
  1.3 44.6 %shard_map.82 = f32[64,1024]{1,0:T(8,128)} custom-call(bf16[64,1024]{1,0:T(8,128)(2,1)} %q_ref.1, bf16[64,2,256]{2,1,0:T(2,128)(2,1)} %seg_hbm.1, bf16[256,2,256]{2,1,0:T(2,128)(2,1)} %fin_hbm.1, bf16[4096,2,256]{2,1,0:T(2,128)(2,1)} %cache_hbm.1, s32[2,32]{1,0:T(2,128)} %mask_ref.1, s32[1]{0:T(128)S(6)} %copy.10.owner_ref, s32[1]{0:T(128)S(6)} %copy.11.valid_ref, ...), custom_call_target="tpu_custom_call" | custom-call | tf_op jit(solution)/shard_map/pallas_call | solution.py:400
  45.9 1.7 %copy.12 = f32[64,1024]{1,0:T(8,128)} copy(f32[64,1024]{1,0:T(8,128)} %shard_map.82) | data formatting | bytes 524288
